TPU v7x, 256 devices: a whole 4x4x8 slice. The times are simulated.
256 devices in a mesh: batch: 2 (over x_hi), ctx: 128 (over y, z, x_lo, core).
Axes of the slice: x: 4 (x_hi: 2, x_lo: 2; x = x_hi * 2 + x_lo), y: 4, z: 8, core: 2. Of those that a mesh axis runs over, the one named last changes fastest.
Arguments:
- queries: bfloat16 [1024, 4096], P(('batch', 'ctx')), parts along dimension 0, may hold values from -24 to 24
- owners: int32 [512, 1], P('batch'), parts along dimension 0, may hold values from 0 to 127; in each aligned block of 256 rows (0 to 255, 256 to 511, ...) at most 4 rows name the same one
- new_keys: bfloat16 [1024, 1024], P(('batch', 'ctx')), parts along dimension 0, may hold values from -6 to 6
- new_values: bfloat16 [1024, 1024], P(('batch', 'ctx')), parts along dimension 0, may hold values from -6 to 6
- cache_keys: bfloat16 [65536, 1024], P(('batch', 'ctx')), parts along dimension 0, may hold values from -16 to 16
- cache_values: bfloat16 [65536, 1024], P(('batch', 'ctx')), parts along dimension 0, may hold values from -6 to 6
- lengths: int32 [256], P(('batch', 'ctx')), parts along dimension 0, may hold values from 1 to 256, as said below
Outputs:
- attended: bfloat16 [1024, 4096], P(('batch', 'ctx')), parts along dimension 0
There are 2 independent parts, one for each index of `batch`. A program takes and returns all parts, laid end to end along the dimension named above; each array names one. Nothing has to cross between parts.
Inputs may be any that keep to these rules, and one draw needn't show every extreme that they name: `owners`: at most 4 new tokens on one device, exactly 4 on some device. `lengths`: the live slots of a device are its first ones; some device is full.
All inputs are finite; a program needn't handle non-finite values.
Results may differ from a plain program's by a relative error of at most 0.003.
Values may be sent and summed in bfloat16 or wider, within the bound.
No kernel may reach another device: no remote copies, remote signals or barrier semaphores. Data moves between devices by JAX's collectives and lax.ppermute only.
A program may use at most 128 MiB of HBM per device.

v0:
```python
import math

import jax
import jax.numpy as jnp
from jax import lax
from jax.sharding import PartitionSpec as P

QUERY_HEADS = 32
KEY_VALUE_HEADS = 8
HEAD_DIMENSION = 128


def slot_tokens(owners, count, slots):
    owner_col = owners[:, 0]
    devices = jnp.arange(count, dtype=jnp.int32)
    onehot = (owner_col[:, None] == devices[None, :]).astype(jnp.int32)
    earlier = jnp.cumsum(onehot, axis=0) - onehot
    rank = jnp.sum(earlier * onehot, axis=1)
    placed = owner_col * slots + rank
    tokens = jnp.arange(owner_col.shape[0], dtype=jnp.int32)
    return jnp.full((count * slots,), -1, jnp.int32).at[placed].set(tokens)


def block_terms(queries, query_tokens, keys, value_rows, live, new_keys, new_values, new_tokens):
    query_rows = queries.shape[0]
    head_group = QUERY_HEADS // KEY_VALUE_HEADS
    scale = 1.0 / math.sqrt(HEAD_DIMENSION)
    cache_mask = (jnp.arange(keys.shape[0], dtype=jnp.int32) < live)[None, None, :]
    new_mask = ((new_tokens[None, :] >= 0) & (new_tokens[None, :] <= query_tokens[:, None]))[
        :, None, :
    ]
    outputs, peaks, totals = ([], [], [])
    for head_index in range(KEY_VALUE_HEADS):
        query = queries[
            :,
            head_index
            * head_group
            * HEAD_DIMENSION : (head_index + 1)
            * head_group
            * HEAD_DIMENSION,
        ].reshape(query_rows, head_group, HEAD_DIMENSION)
        key_old = keys[:, head_index * HEAD_DIMENSION : (head_index + 1) * HEAD_DIMENSION]
        value_old = value_rows[:, head_index * HEAD_DIMENSION : (head_index + 1) * HEAD_DIMENSION]
        key_new = new_keys[:, head_index * HEAD_DIMENSION : (head_index + 1) * HEAD_DIMENSION]
        value_new = new_values[:, head_index * HEAD_DIMENSION : (head_index + 1) * HEAD_DIMENSION]
        score_old = (
            jnp.einsum("rhd,kd->rhk", query, key_old, preferred_element_type=jnp.float32) * scale
        )
        score_new = (
            jnp.einsum("rhd,kd->rhk", query, key_new, preferred_element_type=jnp.float32) * scale
        )
        score_old = jnp.where(cache_mask, score_old, -1e30)
        score_new = jnp.where(new_mask, score_new, -1e30)
        peak = jnp.maximum(jnp.max(score_old, axis=-1), jnp.max(score_new, axis=-1))
        weight_old = jnp.where(cache_mask, jnp.exp(score_old - peak[..., None]), 0.0)
        weight_new = jnp.where(new_mask, jnp.exp(score_new - peak[..., None]), 0.0)
        total = jnp.sum(weight_old, axis=-1) + jnp.sum(weight_new, axis=-1)
        mixed = jnp.einsum(
            "rhk,kd->rhd",
            weight_old.astype(jnp.bfloat16),
            value_old,
            preferred_element_type=jnp.float32,
        )
        mixed = mixed + jnp.einsum(
            "rhk,kd->rhd",
            weight_new.astype(jnp.bfloat16),
            value_new,
            preferred_element_type=jnp.float32,
        )
        outputs.append(mixed)
        peaks.append(peak)
        totals.append(total)
    combined = jnp.concatenate(outputs, axis=1).reshape(query_rows, QUERY_HEADS * HEAD_DIMENSION)
    return (combined, jnp.concatenate(peaks, axis=1), jnp.concatenate(totals, axis=1))


def per_device(queries, owners, new_keys, new_values, cache_keys, cache_values, lengths):
    count = lax.axis_size("ctx")
    here = lax.axis_index("ctx")
    slots = queries.shape[0]
    tokens = slot_tokens(owners, count, slots)
    mine = lax.dynamic_slice_in_dim(tokens, here * slots, slots)
    live = lengths[0]
    everyone = lax.all_gather(queries, "ctx", axis=0, tiled=True)
    weighted, block_max, block_sum = block_terms(
        everyone, tokens, cache_keys, cache_values, live, new_keys, new_values, mine
    )
    overall = lax.pmax(block_max.astype(jnp.bfloat16), "ctx").astype(block_max.dtype)
    factor = jnp.exp(block_max - overall)
    width = everyone.shape[0]
    scaled = (weighted.reshape(width, QUERY_HEADS, HEAD_DIMENSION) * factor[..., None]).reshape(
        width, QUERY_HEADS * HEAD_DIMENSION
    )
    gathered_out, gathered_sum = (
        lax.psum_scatter(scaled, "ctx", scatter_dimension=0, tiled=True),
        lax.psum_scatter(block_sum * factor, "ctx", scatter_dimension=0, tiled=True),
    )
    result = (
        gathered_out.reshape(slots, QUERY_HEADS, HEAD_DIMENSION) / gathered_sum[..., None]
    ).reshape(slots, QUERY_HEADS * HEAD_DIMENSION)
    result = jnp.where(mine[:, None] >= 0, result, 0.0)
    return result.astype(jnp.bfloat16)


def solution(mesh):
    return jax.shard_map(
        per_device,
        mesh=mesh,
        in_specs=(
            P(("batch", "ctx"), None),
            P("batch", None),
            P(("batch", "ctx"), None),
            P(("batch", "ctx"), None),
            P(("batch", "ctx"), None),
            P(("batch", "ctx"), None),
            P(("batch", "ctx")),
        ),
        out_specs=P(("batch", "ctx"), None),
        check_vma=False,
    )
```

profile of v0, /device:TPU:1, one launch (start us, length us, event | category | flops | bytes accessed | tf_op | source)
XLA Modules:
  0.0 1960.9 jit_solution(10898466710654283034)
XLA Ops:
  10.6 1.4 scatter_custom_fusion
  12.2 216.2 %all-gather.3.cloned.1.call-done = bf16[128,4,4096]{2,1,0:T(4,128)(2,1)} async-done(((bf16[1,4,4096]{2,1,0:T(4,128)(2,1)}), bf16[128,4,4096]{2,1,0:T(4,128)(2,1)}) %all-gather.3.cloned.1.call-update) | async-done | bytes 4194320 | tf_op jit(solution)/shard_map/all_gather | solution.py:84
  228.4 6.9 reshape.150
  235.3 3.8 fusion.256
  240.2 2.6 fusion.122
  242.8 1.3 fusion.118
  244.0 1.3 copy.125
  245.5 2.6 fusion.116
  248.1 1.3 copy.130
  249.5 2.6 fusion.114
  252.1 1.3 copy.135
  253.6 2.6 fusion.112
  256.2 1.3 copy.140
  257.7 2.7 fusion.110
  260.3 1.3 copy.145
  262.8 1.2 fusion.259
  264.1 2.5 fusion.7
  266.7 1.7 fusion.54
  270.2 5.0 fusion.22
  275.2 1.7 fusion.48
  276.9 1.9 fusion.46
  278.8 1.7 fusion.50
  280.5 1.7 fusion.44
  282.2 1.7 fusion.52
  283.9 3.3 fusion.20
  287.3 2.4 fusion.42
  289.8 544.9 %pmax.7 = bf16[512,32]{0,1:T(8,128)(2,1)S(1)} all-reduce(bf16[512,32]{0,1:T(8,128)(2,1)S(1)} %convert_element_type.82), channel_id=1, replica_groups=mesh['batch'=2,'ctx'=128] {'ctx'}, use_global_device_ids=true, to_apply=%region_20.21 | all-reduce | flops 16384 | bytes 65536 | tf_op jit(solution)/shard_map/pmax | solution.py:88
  836.3 1.7 fusion.30
  841.2 4.4 broadcast_multiply_fusion
  845.6 8.9 copy.150
  856.4 1095.0 %all-reduce.5.cloned.1.call-done = (f32[512,32]{0,1:T(8,128)}, f32[512,4096]{1,0:T(8,128)}) async-done(((f32[512,32]{0,1:T(8,128)}, f32[512,4096]{1,0:T(8,128)}), (f32[512,32]{0,1:T(8,128)}, f32[512,4096]{1,0:T(8,128)})) %all-reduce.5.cloned.1.call-update) | async-done | bytes 8454160
  1952.4 1.6 select_convert_fusion
  (95 shorter events, 15.4 us)
Async XLA Ops:
  6.5 221.8 %all-gather.3.cloned.1.call-start = ((), (), s32[]{:S(2)}) async-start(), calls=%async_computation | async-start | bytes 4227072 | tf_op jit(solution)/shard_map/all_gather | solution.py:84
  7.3 1944.2 %all-reduce.5.cloned.1.call-start = ((), (), s32[]{:S(2)}) async-start(), calls=%async_computation.1 | async-start | bytes 16908288
  12.0 271.9 %copy-start.14 = (pred[256]{0:T(512)(128)(4,1)}, pred[256]{0:T(512)(128)(4,1)S(1)}, u32[]{:S(2)}) copy-start(pred[256]{0:T(512)(128)(4,1)S(1)} %iota_compare_fusion.1) | copy-start | bytes 772
  239.1 0.7 copy-start.12
  264.1 2.6 copy-start.4
  264.1 2.6 copy-start.15
  264.1 5.0 copy-start.3
  266.7 2.4 copy-start.1
  266.7 2.7 copy-start.2
  268.4 1.7 copy-start
  268.4 1.8 copy-start.5
  287.3 548.6 %copy-start.6 = (f32[512,4,128]{0,2,1:T(8,128)S(1)}, f32[512,4,128]{0,2,1:T(8,128)}, u32[]{:S(2)}) copy-start(f32[512,4,128]{0,2,1:T(8,128)} %fusion.54) | copy-start | bytes 3145732
  287.3 548.6 %copy-start.13 = (bf16[4,1024]{1,0:T(4,128)(2,1)S(1)}, bf16[4,1024]{1,0:T(4,128)(2,1)}, u32[]{:S(2)}) copy-start(bf16[4,1024]{1,0:T(4,128)(2,1)} %param.10) | copy-start | bytes 24580
  835.9 2.1 copy-start.10
  836.2 2.1 copy-start.8
  837.9 1.2 copy-start.7
  838.3 1.3 copy-start.9
  839.2 1.3 copy-start.11
  854.5 0.7 copy-start.16
Sparse Core Ops, SparseCore 0:
  9.2 219.1 all-gather.2
  854.6 1096.7 all-reduce.4
where the time goes:
time: 1960 us
  waiting for transfers between devices  1310 us (67%)
  blocking collectives  545 us (28%)
  matrix products  42.2 us (2%)
  local copies, waits for them, and re-layouts  34.3 us (2%)
    unnamed x3, waiting for transfers between devices  1100 us
    pmax x1, blocking collectives, per_device(): lax.pmax(block_max.astype(jnp.bfloat16), 'ctx').astype(block_max.dtype)  545 us
    all_gather x1, waiting for transfers between devices, per_device(): everyone = lax.all_gather(queries, 'ctx', axis=0, tiled=True)  216 us
  transfers between devices with their start and end apart: 2, of which 2 were waited for; matrix products, arithmetic and copies ran while one was open for 0% of the time, Pallas kernels for 0%

commit v1 on v0

v1 whole, which is shorter than its diff:
```python
import math

import jax
import jax.numpy as jnp
from jax import lax
from jax.experimental import pallas as pl
from jax.experimental.pallas import tpu as pltpu
from jax.sharding import PartitionSpec as P

HEAD = 128
KV_HEADS = 8
SLOTS = 4
TOKENS = 256
KEYS = 256
DEVICES = 128
CHIP_MASKS = tuple((d >> 1) * 32 + (d & 1) * 2 for d in range(8))
PIECE = 2 * KEYS + 32
CHUNKS = 17
SCALE = math.log2(math.e) / math.sqrt(HEAD)
HIDDEN = -1e30


def swap(array, mask):
    return lax.ppermute(array, "ctx", [(i, i ^ mask) for i in range(DEVICES)])


def pack_kernel(head_ref, live_ref, queries, new_keys, new_values, keys, values, send, *rest):
    pieces, tail = rest[:8], rest[8]
    f32, bf16 = jnp.float32, jnp.bfloat16
    for y in range(4):
        for z in range(8):
            for low in range(4):
                at = (4 * y + low) * 256
                send[32 * y + 4 * z + low] = queries[:, at : at + 256]
    width = KV_HEADS * HEAD
    live = jnp.full((8, width), live_ref[0].astype(f32))
    gap = jnp.zeros((4, width), f32)
    tail[0:16, :] = jnp.concatenate([new_keys[...].astype(f32), gap, live], axis=0).astype(bf16)
    tail[16:32, :] = jnp.concatenate([new_values[...].astype(f32), gap, gap, gap], axis=0).astype(bf16)
    head = head_ref[0]
    for d in range(8):
        column = pl.ds(pl.multiple_of((head ^ d) * HEAD, HEAD), HEAD)
        pieces[d][0:KEYS, :] = keys[:, column]
        pieces[d][KEYS : 2 * KEYS, :] = values[:, column]
        pieces[d][2 * KEYS : PIECE, :] = tail[:, column]


def pack(head, live, queries, new_keys, new_values, keys, values):
    whole = pl.BlockSpec(memory_space=pltpu.VMEM)
    return pl.pallas_call(
        pack_kernel,
        out_shape=[jax.ShapeDtypeStruct((DEVICES, SLOTS, 256), jnp.bfloat16)]
        + [jax.ShapeDtypeStruct((PIECE, HEAD), jnp.bfloat16)] * 8,
        in_specs=[pl.BlockSpec(memory_space=pltpu.SMEM)] * 2 + [whole] * 5,
        out_specs=[whole] * 9,
        scratch_shapes=[pltpu.VMEM((32, KV_HEADS * HEAD), jnp.bfloat16)],
        cost_estimate=pl.CostEstimate(flops=0, bytes_accessed=2 << 20, transcendentals=0),
        name="pack",
    )(head, live, queries, new_keys, new_values, keys, values)


def attend_kernel(here_ref, q_ref, col_ref, row_ref, *rest):
    pieces, out_ref, scores, new_keys, new_values = rest[:16], rest[16], rest[17], rest[18], rest[19]
    f32, bf16, i32 = jnp.float32, jnp.bfloat16, jnp.int32
    here = here_ref[0]
    iota = lambda shape, dim: lax.broadcasted_iota(i32, shape, dim)
    own_col, own_row = col_ref[...], row_ref[...]

    same = own_col == own_row
    down, across = iota((TOKENS, TOKENS), 0), iota((TOKENS, TOKENS), 1)
    rank_col = jnp.sum(jnp.where(same & (across < down), 1.0, 0.0), axis=1, keepdims=True)
    rank_row = jnp.sum(jnp.where(same & (down < across), 1.0, 0.0), axis=0, keepdims=True)
    place_col = own_col * SLOTS + rank_col.astype(i32)
    place_row = own_row * SLOTS + rank_row.astype(i32)

    pick = jnp.where(place_col == iota((TOKENS, DEVICES * SLOTS), 1), 1.0, 0.0).astype(bf16)
    by_token = jnp.dot(pick, q_ref[...], preferred_element_type=f32).astype(bf16)
    queries = jnp.concatenate([by_token[:, :HEAD], by_token[:, HEAD:]], axis=0)

    contract = (((1,), (1,)), ((), ()))
    lane = iota((1, KEYS), 1).astype(f32)
    peak = jnp.full((2 * TOKENS, HEAD), HIDDEN, f32)
    for p in range(16):
        tail = pieces[p][2 * KEYS : 2 * KEYS + 16, :]
        new_keys[16 * p : 16 * p + 16, :] = tail
        new_values[16 * p : 16 * p + 16, :] = pieces[p][2 * KEYS + 16 : PIECE, :]
        live = tail.astype(f32)[8:9, 0:1]
        bias = jnp.where(lane < live, 0.0, HIDDEN)
        score = lax.dot_general(queries, pieces[p][0:KEYS, :], contract, preferred_element_type=f32)
        score = score * SCALE + bias
        scores[p] = score
        peak = jnp.maximum(peak, jnp.maximum(score[:, :HEAD], score[:, HEAD:]))

    column = iota((1, KEYS), 1)
    part, row = column >> 4, column & 15
    device = here ^ (((part >> 1) & 3) * 32 + (part & 1) * 2 + (part >> 3))
    slot = jnp.where(row < SLOTS, device * SLOTS + row, -1)
    match = place_col == slot
    token = jnp.sum(jnp.where(match, iota((TOKENS, KEYS), 0).astype(f32) + 1.0, 0.0), axis=0, keepdims=True) - 1.0
    reader = iota((2 * TOKENS, 1), 0)
    reader = jnp.where(reader >= TOKENS, reader - TOKENS, reader).astype(f32)
    seen = (token >= 0.0) & (token <= reader)
    score = lax.dot_general(queries, new_keys[...], contract, preferred_element_type=f32)
    score = jnp.where(seen, score * SCALE, HIDDEN)
    scores[16] = score
    peak = jnp.maximum(peak, jnp.maximum(score[:, :HEAD], score[:, HEAD:]))

    peak = jnp.max(peak, axis=1, keepdims=True)
    total = jnp.zeros((2 * TOKENS, HEAD), f32)
    mixed = jnp.zeros((2 * TOKENS, HEAD), f32)
    for p in range(CHUNKS):
        weight = jnp.exp2(scores[p] - peak)
        total = total + (weight[:, :HEAD] + weight[:, HEAD:])
        value = new_values[...] if p == 16 else pieces[p][KEYS : 2 * KEYS, :]
        mixed = mixed + jnp.dot(weight.astype(bf16), value, preferred_element_type=f32)
    total = jnp.sum(total, axis=1, keepdims=True)
    mean = mixed / total

    step = jnp.round(jnp.log2(jnp.maximum(jnp.max(jnp.abs(mean), axis=1, keepdims=True), 1e-30)))
    mean = mean * jnp.exp2(-step)
    rough = mean.astype(bf16)
    rest_of_mean = (mean - rough.astype(f32)).astype(bf16)
    level = peak + jnp.log2(total)
    high = level.astype(bf16).astype(f32)
    middle = (level - high).astype(bf16).astype(f32)
    low = level - high - middle
    lanes = iota((TOKENS, HEAD), 1)
    place = lanes & 63
    parts = jnp.zeros((TOKENS, HEAD), f32)
    for number, part in enumerate((high, middle, low, step)):
        parts = jnp.where(place == 2 * number, part[:TOKENS], parts)
        parts = jnp.where(place == 2 * number + 1, part[TOKENS:], parts)
    rows = jnp.concatenate(
        [rough[:TOKENS], rough[TOKENS:], rest_of_mean[:TOKENS], rest_of_mean[TOKENS:], parts.astype(bf16)],
        axis=1,
    )

    line = iota((TOKENS, TOKENS), 0) * 2
    even = jnp.where(line == place_row, 1.0, 0.0).astype(bf16)
    odd = jnp.where(line + 1 == place_row, 1.0, 0.0).astype(bf16)
    first = jnp.dot(even, rows, preferred_element_type=f32)
    second = jnp.dot(odd, rows, preferred_element_type=f32)
    out_ref[:, 0:256] = first[:, 0:256] + first[:, 256:512]
    out_ref[:, 256:512] = second[:, 0:256] + second[:, 256:512]
    out_ref[:, 512:640] = jnp.where(lanes < 64, first[:, 512:], second[:, 512:])


def attend(here, queries, own_col, own_row, pieces):
    whole = pl.BlockSpec(memory_space=pltpu.VMEM)
    return pl.pallas_call(
        attend_kernel,
        out_shape=jax.ShapeDtypeStruct((TOKENS, 640), jnp.float32),
        in_specs=[pl.BlockSpec(memory_space=pltpu.SMEM)] + [whole] * 19,
        out_specs=whole,
        scratch_shapes=[
            pltpu.VMEM((CHUNKS, 2 * TOKENS, KEYS), jnp.float32),
            pltpu.VMEM((KEYS, HEAD), jnp.bfloat16),
            pltpu.VMEM((KEYS, HEAD), jnp.bfloat16),
        ],
        compiler_params=pltpu.CompilerParams(vmem_limit_bytes=40 << 20),
        cost_estimate=pl.CostEstimate(
            flops=4 * 512 * 4352 * 128, bytes_accessed=3 << 20, transcendentals=512 * 4352
        ),
        name="attend",
    )(here, queries, own_col, own_row, *pieces)


def combine_kernel(parts_ref, out_ref):
    rows = parts_ref[...]
    levels = rows[:, 512:640]
    for v in range(4):
        at = 64 * (v // 2) + v % 2
        level = levels[:, at : at + 1] + levels[:, at + 2 : at + 3] + levels[:, at + 4 : at + 5]
        level = level.reshape(4, 8, 8, 1)
        factor = jnp.exp2(level - jnp.max(level, axis=1, keepdims=True))
        step = jnp.exp2(levels[:, at + 6 : at + 7]).reshape(4, 8, 8, 1)
        mean = rows[:, v * HEAD : (v + 1) * HEAD].reshape(4, 8, 8, HEAD)
        whole = jnp.sum(mean * (factor * step), axis=1) / jnp.sum(factor, axis=1)
        out_ref[:, v * HEAD : (v + 1) * HEAD] = whole.reshape(32, HEAD)


def combine(parts):
    whole = pl.BlockSpec(memory_space=pltpu.VMEM)
    return pl.pallas_call(
        combine_kernel,
        out_shape=jax.ShapeDtypeStruct((32, 512), jnp.float32),
        in_specs=[whole],
        out_specs=whole,
        name="combine",
    )(parts)


def per_device(queries, owners, new_keys, new_values, cache_keys, cache_values, lengths):
    bf16 = jnp.bfloat16
    here = lax.axis_index("ctx").astype(jnp.int32)
    head = (here >> 5) * 2 + ((here >> 1) & 1)

    send, *mine = pack(head[None], lengths, queries, new_keys, new_values, cache_keys, cache_values)
    everyone = lax.all_to_all(send, "ctx", 0, 0).reshape(DEVICES * SLOTS, 256)
    held = [mine[0]] + [swap(mine[d], CHIP_MASKS[d]) for d in range(1, 8)]
    other = [swap(piece, 1) for piece in held]

    partial = attend(here[None], everyone, owners, owners.reshape(1, TOKENS), held + other)
    spread = lax.all_to_all(partial.astype(jnp.float16).reshape(DEVICES, 2, 640), "ctx", 0, 0)
    result = combine(spread.astype(jnp.float32).reshape(2 * DEVICES, 640))
    result = result.reshape(16, 2, 2, 256).transpose(1, 2, 0, 3).reshape(SLOTS, 4096)
    return result.astype(bf16)


def solution(mesh):
    return jax.shard_map(
        per_device,
        mesh=mesh,
        in_specs=(
            P(("batch", "ctx"), None),
            P("batch", None),
            P(("batch", "ctx"), None),
            P(("batch", "ctx"), None),
            P(("batch", "ctx"), None),
            P(("batch", "ctx"), None),
            P(("batch", "ctx")),
        ),
        out_specs=P(("batch", "ctx"), None),
        check_vma=False,
    )
```

time: 1960 us -> 82.9 us (0.04)
  waiting for transfers between devices: 1310 us -> 2.47 us
  blocking collectives: 545 us -> 25.2 us
  matrix products: 42.2 us -> 0 us
  starting transfers between devices: 0.04 us -> 39.1 us
  local copies, waits for them, and re-layouts: 34.3 us -> 2.34 us
    unnamed x3 -> x0, waiting for transfers between devices: 1100 us -> none
    pmax x1 -> x0, blocking collectives: 545 us -> none  [per_device(): lax.pmax(block_max.astype(jnp.bfloat16), 'ctx').astype(block_max.dtype)]
    all_gather x1 -> x0, waiting for transfers between devices: 216 us -> none  [per_device(): everyone = lax.all_gather(queries, 'ctx', axis=0, tiled=True)]
    dot_general x32 -> x0, matrix products: 42.2 us -> none  [the longest x8 21.8 us: block_terms(): jnp.einsum('rhd,kd->rhk', query, key_old, preferred_element_type=jnp.floa...]
    all_to_all x0 -> x1, blocking collectives: none -> 25.2 us  [per_device(): lax.all_to_all(partial.astype(jnp.float16).reshape(DEVICES, 2, 640), 'ctx...]
    ppermute x0 -> x15, starting transfers between devices: none -> 24.1 us  [swap(): return lax.ppermute(array, 'ctx', [(i, i ^ mask) for i in range(DEVICES)])]
  transfers between devices with their start and end apart: 2 -> 16, of which waited for: 2 -> 6; matrix products, arithmetic and copies ran while one was open for 0% -> 0% of each run, Pallas kernels for 0% -> 0%
where the time goes in v1:
time: 82.9 us; the launch traced here: 82.6 us
  starting transfers between devices  39.1 us (47%)
  blocking collectives  25.2 us (30%)
  Pallas kernels  11.6 us (14%)
  waiting for transfers between devices  2.47 us (3%)
  local copies, waits for them, and re-layouts  2.34 us (3%)
  other arithmetic  1.11 us (1%)
    all_to_all x1, blocking collectives, per_device(): lax.all_to_all(partial.astype(jnp.float16).reshape(DEVICES, 2, 640), 'ctx...  25.2 us
    ppermute x15, starting transfers between devices, swap(): return lax.ppermute(array, 'ctx', [(i, i ^ mask) for i in range(DEVICES)])  24.1 us
    all_to_all x1, starting transfers between devices, per_device(): everyone = lax.all_to_all(send, 'ctx', 0, 0).reshape(DEVICES * SLOTS, 256)  15 us
    pallas_call x1, Pallas kernels, attend(): pl.pallas_call(attend_kernel, out_shape=jax.ShapeDtypeStruct((TOKENS, 640...  7.09 us
    ppermute x15, waiting for transfers between devices, swap(): return lax.ppermute(array, 'ctx', [(i, i ^ mask) for i in range(DEVICES)])  2.47 us
    pallas_call x1, Pallas kernels, pack(): pl.pallas_call(pack_kernel, out_shape=[jax.ShapeDtypeStruct((DEVICES, SLO...  2.47 us
    pallas_call x1, Pallas kernels, combine(): pl.pallas_call(combine_kernel, out_shape=jax.ShapeDtypeStruct((32, 512),...  2.07 us
  transfers between devices with their start and end apart: 16, of which 6 were waited for; matrix products, arithmetic and copies ran while one was open for 0% of the time, Pallas kernels for 0%

profile of v1, /device:TPU:1, one launch (start us, length us, event | category | flops | bytes accessed | tf_op | source)
XLA Modules:
  0.0 82.6 jit_solution(2769969763462722504)
XLA Ops:
  0.7 2.5 %pack.1 = (bf16[128,4,256]{2,1,0:T(4,128)(2,1)}, bf16[544,128]{1,0:T(8,128)(2,1)}, bf16[544,128]{1,0:T(8,128)(2,1)}, bf16[544,128]{1,0:T(8,128)(2,1)}, bf16[544,...) custom-call(s32[1]{0:T(128)} %bitcast.1.head_ref, ...), custom_call_target="tpu_custom_call" | custom-call | bytes 2097152 | tf_op jit(solution)/shard_map/pack/pallas_call | solution.py:50
  3.1 15.0 %all-to-all-start = ((bf16[128,4,256]{2,1,0:T(4,128)(2,1)}), bf16[128,4,256]{2,1,0:T(4,128)(2,1)S(1)}, u32[]{:S(2)}, u32[]{:S(2)}) async-start(bf16[128,4,256]{2,1,0:T(4,128)(2,1)} %get-tuple-element.14), calls=%async_computation | async-start | bytes 524288 | tf_op jit(solution)/shard_map/all_to_all | solution.py:199
  18.1 1.5 %collective-permute-start = (bf16[544,128]{1,0:T(8,128)(2,1)}, bf16[544,128]{1,0:T(8,128)(2,1)S(1)}, u32[]{:S(2)}, u32[]{:S(2)}) collective-permute-start(bf16[544,128]{1,0:T(8,128)(2,1)} %get-tuple-element.16), channel_id=1, source_target_pairs={{0,2},{1,3},{2,0},{3,1},{4,6},{5,7},{6,4},{7,5},{8,10},{9,11},{10,... | collective-permute-start | bytes 417800 | tf_op jit(solution)/shard_map/ppermute | solution.py:24
  19.6 1.3 %collective-permute-start.1 = (bf16[544,128]{1,0:T(8,128)(2,1)}, bf16[544,128]{1,0:T(8,128)(2,1)S(1)}, u32[]{:S(2)}, u32[]{:S(2)}) collective-permute-start(bf16[544,128]{1,0:T(8,128)(2,1)} %get-tuple-element.17), channel_id=1, source_target_pairs={{0,32},{1,33},{2,34},{3,35},{4,36},{5,37},{6,38},{7,39},{8,40},{9,... | collective-permute-start | bytes 417800 | tf_op jit(solution)/shard_map/ppermute | solution.py:24
  20.9 3.2 %collective-permute-start.3 = (bf16[544,128]{1,0:T(8,128)(2,1)}, bf16[544,128]{1,0:T(8,128)(2,1)S(1)}, u32[]{:S(2)}, u32[]{:S(2)}) collective-permute-start(bf16[544,128]{1,0:T(8,128)(2,1)} %get-tuple-element.19), channel_id=1, source_target_pairs={{0,64},{1,65},{2,66},{3,67},{4,68},{5,69},{6,70},{7,71},{8,72},{9,... | collective-permute-start | bytes 417800 | tf_op jit(solution)/shard_map/ppermute | solution.py:24
  24.1 0.9 %collective-permute-start.4 = (bf16[544,128]{1,0:T(8,128)(2,1)}, bf16[544,128]{1,0:T(8,128)(2,1)S(1)}, u32[]{:S(2)}, u32[]{:S(2)}) collective-permute-start(bf16[544,128]{1,0:T(8,128)(2,1)} %get-tuple-element.20), channel_id=1, source_target_pairs={{0,66},{1,67},{2,64},{3,65},{4,70},{5,71},{6,68},{7,69},{8,74},{9,... | collective-permute-start | bytes 417800 | tf_op jit(solution)/shard_map/ppermute | solution.py:24
  25.0 2.9 %collective-permute-start.5 = (bf16[544,128]{1,0:T(8,128)(2,1)S(1)}, bf16[544,128]{1,0:T(8,128)(2,1)S(1)}, u32[]{:S(2)}, u32[]{:S(2)}) collective-permute-start(bf16[544,128]{1,0:T(8,128)(2,1)S(1)} %copy-done.3), channel_id=1, source_target_pairs={{0,96},{1,97},{2,98},{3,99},{4,100},{5,101},{6,102},{7,103},{8,104... | collective-permute-start | bytes 417800 | tf_op jit(solution)/shard_map/ppermute | solution.py:24
  27.9 1.7 %collective-permute-start.6 = (bf16[544,128]{1,0:T(8,128)(2,1)S(1)}, bf16[544,128]{1,0:T(8,128)(2,1)S(1)}, u32[]{:S(2)}, u32[]{:S(2)}) collective-permute-start(bf16[544,128]{1,0:T(8,128)(2,1)S(1)} %copy-done.2), channel_id=1, source_target_pairs={{0,98},{1,99},{2,96},{3,97},{4,102},{5,103},{6,100},{7,101},{8,106... | collective-permute-start | bytes 417800 | tf_op jit(solution)/shard_map/ppermute | solution.py:24
  29.6 0.3 collective-permute-done.2.rest_3_
  29.9 8.1 %collective-permute-start.7 = (bf16[544,128]{1,0:T(8,128)(2,1)S(1)}, bf16[544,128]{1,0:T(8,128)(2,1)S(1)}, u32[]{:S(2)}, u32[]{:S(2)}) collective-permute-start(bf16[544,128]{1,0:T(8,128)(2,1)S(1)} %copy-done.1), channel_id=1, source_target_pairs={{0,1},{1,0},{2,3},{3,2},{4,5},{5,4},{6,7},{7,6},{8,9},{9,8},{10,11... | collective-permute-start | bytes 417800 | tf_op jit(solution)/shard_map/ppermute | solution.py:24
  38.0 1.3 %collective-permute-done.3.rest_4_ = bf16[544,128]{1,0:T(8,128)(2,1)S(1)} collective-permute-done((bf16[544,128]{1,0:T(8,128)(2,1)}, bf16[544,128]{1,0:T(8,128)(2,1)S(1)}, u32[]{:S(2)}, u32[]{:S(2)}) %collective-permute-start.3) | collective-permute-done | bytes 139296 | tf_op jit(solution)/shard_map/ppermute | solution.py:24
  39.3 1.1 %collective-permute-start.8 = (bf16[544,128]{1,0:T(8,128)(2,1)S(1)}, bf16[544,128]{1,0:T(8,128)(2,1)S(1)}, u32[]{:S(2)}, u32[]{:S(2)}) collective-permute-start(bf16[544,128]{1,0:T(8,128)(2,1)S(1)} %collective-permute-done.rest_1_), channel_id=1, source_target_pairs={{0,1},{1,0},{2,3},{3,2},{4,5},{5,4},{6,7},{7,6},{8,9},{9,8},{10,11... | collective-permute-start | bytes 417800 | tf_op jit(solution)/shard_map/ppermute | solution.py:24
  40.4 0.0 collective-permute-start.9
  40.4 2.4 %collective-permute-start.10 = (bf16[544,128]{1,0:T(8,128)(2,1)S(1)}, bf16[544,128]{1,0:T(8,128)(2,1)S(1)}, u32[]{:S(2)}, u32[]{:S(2)}) collective-permute-start(bf16[544,128]{1,0:T(8,128)(2,1)S(1)} %collective-permute-done.2.rest_3_), channel_id=1, source_target_pairs={{0,1},{1,0},{2,3},{3,2},{4,5},{5,4},{6,7},{7,6},{8,9},{9,8},{10,11... | collective-permute-start | bytes 417800 | tf_op jit(solution)/shard_map/ppermute | solution.py:24
  42.8 0.0 collective-permute-start.11
  42.9 0.5 collective-permute-start.12
  43.4 0.1 collective-permute-start.13
  43.5 0.4 collective-permute-start.14
  43.9 0.1 copy.8.col_ref
  44.0 0.1 reshape.18.q_ref
  44.1 0.1 collective-permute-done.11.rest_12_
  44.2 0.2 collective-permute-done.12.rest_13_
  44.4 0.3 collective-permute-done.13.rest_14_
  44.7 0.3 collective-permute-done.14.rest_15_
  45.0 7.1 %attend.1 = f32[256,640]{1,0:T(8,128)S(1)} custom-call(s32[1]{0:T(128)} %bitcast.here_ref, bf16[512,256]{1,0:T(8,128)(2,1)S(1)} %reshape.18.q_ref, s32[256,1]{1,0:T(8,128)S(1)} %copy.8.col_ref, s32[1,256]{1,0:T(1,128)S(1)} %bitcast.7, bf16[544,128]{1,0:T(8,128)(2,1)S(1)} %copy-done.1, bf16[544,128]{1,0:T(8,128)(2,1)S(1)} %collective-permute-done.rest_1_, ...), custom_call_target="tpu_custom_call" | custom-call | flops 1140850688 | bytes 3145728 | tf_op jit(solution)/shard_map/attend/pallas_call | solution.py:150
  52.1 0.2 reshape.20
  52.3 25.2 %all_to_all.10 = f16[128,2,640]{2,1,0:T(2,128)(2,1)S(1)} all-to-all(f16[128,2,640]{2,1,0:T(2,128)(2,1)S(1)} %reshape.20), channel_id=1, replica_groups=mesh['batch'=2,'ctx'=128] {'ctx'}, dimensions={0} | all-to-all | bytes 655360 | tf_op jit(solution)/shard_map/all_to_all | solution.py:204
  77.5 0.2 reshape.23
  77.7 1.3 %reshape.24.parts_ref = f32[256,640]{1,0:T(8,128)} reshape(f32[128,2,640]{2,1,0:T(2,128)S(1)} %reshape.23) | data formatting | bytes 1310720 | tf_op jit(solution)/shard_map/reshape | solution.py:205
  79.1 2.1 %combine.1 = f32[32,512]{1,0:T(8,128)} custom-call(f32[256,640]{1,0:T(8,128)} %reshape.24.parts_ref), custom_call_target="tpu_custom_call" | custom-call | tf_op jit(solution)/shard_map/combine/pallas_call | solution.py:184
  81.1 0.8 %convert_element_type.17 = bf16[32,512]{1,0:T(8,128)(2,1)S(1)} convert(f32[32,512]{1,0:T(8,128)} %combine.1) | non-fusion elementwise | flops 16384 | bytes 98304 | tf_op jit(solution)/shard_map/convert_element_type | solution.py:207
  82.0 0.6 copy.10
  (22 shorter events, 0.1 us)
Async XLA Ops:
  3.1 21.9 %copy-start.3 = (bf16[544,128]{1,0:T(8,128)(2,1)S(1)}, bf16[544,128]{1,0:T(8,128)(2,1)}, u32[]{:S(2)}) copy-start(bf16[544,128]{1,0:T(8,128)(2,1)} %get-tuple-element.21) | copy-start | bytes 417796
  3.1 24.8 %copy-start.2 = (bf16[544,128]{1,0:T(8,128)(2,1)S(1)}, bf16[544,128]{1,0:T(8,128)(2,1)}, u32[]{:S(2)}) copy-start(bf16[544,128]{1,0:T(8,128)(2,1)} %get-tuple-element.22) | copy-start | bytes 417796
  3.1 26.7 %copy-start.1 = (bf16[544,128]{1,0:T(8,128)(2,1)S(1)}, bf16[544,128]{1,0:T(8,128)(2,1)}, u32[]{:S(2)}) copy-start(bf16[544,128]{1,0:T(8,128)(2,1)} %get-tuple-element.15.rest_0_) | copy-start | bytes 417796
  3.1 40.9 %all-to-all-start = ((bf16[128,4,256]{2,1,0:T(4,128)(2,1)}), bf16[128,4,256]{2,1,0:T(4,128)(2,1)S(1)}, u32[]{:S(2)}, u32[]{:S(2)}) async-start(bf16[128,4,256]{2,1,0:T(4,128)(2,1)} %get-tuple-element.14), calls=%async_computation | async-start | bytes 524288 | tf_op jit(solution)/shard_map/all_to_all | solution.py:199
  18.1 6.9 %collective-permute-start = (bf16[544,128]{1,0:T(8,128)(2,1)}, bf16[544,128]{1,0:T(8,128)(2,1)S(1)}, u32[]{:S(2)}, u32[]{:S(2)}) collective-permute-start(bf16[544,128]{1,0:T(8,128)(2,1)} %get-tuple-element.16), channel_id=1, source_target_pairs={{0,2},{1,3},{2,0},{3,1},{4,6},{5,7},{6,4},{7,5},{8,10},{9,11},{10,... | collective-permute-start | bytes 417800 | tf_op jit(solution)/shard_map/ppermute | solution.py:24
  19.6 8.3 %collective-permute-start.1 = (bf16[544,128]{1,0:T(8,128)(2,1)}, bf16[544,128]{1,0:T(8,128)(2,1)S(1)}, u32[]{:S(2)}, u32[]{:S(2)}) collective-permute-start(bf16[544,128]{1,0:T(8,128)(2,1)} %get-tuple-element.17), channel_id=1, source_target_pairs={{0,32},{1,33},{2,34},{3,35},{4,36},{5,37},{6,38},{7,39},{8,40},{9,... | collective-permute-start | bytes 417800 | tf_op jit(solution)/shard_map/ppermute | solution.py:24
  20.9 8.9 %collective-permute-start.2 = (bf16[544,128]{1,0:T(8,128)(2,1)}, bf16[544,128]{1,0:T(8,128)(2,1)S(1)}, u32[]{:S(2)}, u32[]{:S(2)}) collective-permute-start(bf16[544,128]{1,0:T(8,128)(2,1)} %get-tuple-element.18), channel_id=1, source_target_pairs={{0,34},{1,35},{2,32},{3,33},{4,38},{5,39},{6,36},{7,37},{8,42},{9,... | collective-permute-start | bytes 417800 | tf_op jit(solution)/shard_map/ppermute | solution.py:24
  20.9 18.4 %collective-permute-start.3 = (bf16[544,128]{1,0:T(8,128)(2,1)}, bf16[544,128]{1,0:T(8,128)(2,1)S(1)}, u32[]{:S(2)}, u32[]{:S(2)}) collective-permute-start(bf16[544,128]{1,0:T(8,128)(2,1)} %get-tuple-element.19), channel_id=1, source_target_pairs={{0,64},{1,65},{2,66},{3,67},{4,68},{5,69},{6,70},{7,71},{8,72},{9,... | collective-permute-start | bytes 417800 | tf_op jit(solution)/shard_map/ppermute | solution.py:24
  24.1 16.3 %collective-permute-start.4 = (bf16[544,128]{1,0:T(8,128)(2,1)}, bf16[544,128]{1,0:T(8,128)(2,1)S(1)}, u32[]{:S(2)}, u32[]{:S(2)}) collective-permute-start(bf16[544,128]{1,0:T(8,128)(2,1)} %get-tuple-element.20), channel_id=1, source_target_pairs={{0,66},{1,67},{2,64},{3,65},{4,70},{5,71},{6,68},{7,69},{8,74},{9,... | collective-permute-start | bytes 417800 | tf_op jit(solution)/shard_map/ppermute | solution.py:24
  25.0 15.4 %collective-permute-start.5 = (bf16[544,128]{1,0:T(8,128)(2,1)S(1)}, bf16[544,128]{1,0:T(8,128)(2,1)S(1)}, u32[]{:S(2)}, u32[]{:S(2)}) collective-permute-start(bf16[544,128]{1,0:T(8,128)(2,1)S(1)} %copy-done.3), channel_id=1, source_target_pairs={{0,96},{1,97},{2,98},{3,99},{4,100},{5,101},{6,102},{7,103},{8,104... | collective-permute-start | bytes 417800 | tf_op jit(solution)/shard_map/ppermute | solution.py:24
  27.9 16.0 %copy-start = (s32[256,1]{0,1:T(1,128)S(1)}, s32[256,1]{0,1:T(1,128)}, u32[]{:S(2)}) copy-start(s32[256,1]{0,1:T(1,128)} %param.8) | copy-start | bytes 3076
  27.9 14.9 %collective-permute-start.6 = (bf16[544,128]{1,0:T(8,128)(2,1)S(1)}, bf16[544,128]{1,0:T(8,128)(2,1)S(1)}, u32[]{:S(2)}, u32[]{:S(2)}) collective-permute-start(bf16[544,128]{1,0:T(8,128)(2,1)S(1)} %copy-done.2), channel_id=1, source_target_pairs={{0,98},{1,99},{2,96},{3,97},{4,102},{5,103},{6,100},{7,101},{8,106... | collective-permute-start | bytes 417800 | tf_op jit(solution)/shard_map/ppermute | solution.py:24
  29.9 13.0 %collective-permute-start.7 = (bf16[544,128]{1,0:T(8,128)(2,1)S(1)}, bf16[544,128]{1,0:T(8,128)(2,1)S(1)}, u32[]{:S(2)}, u32[]{:S(2)}) collective-permute-start(bf16[544,128]{1,0:T(8,128)(2,1)S(1)} %copy-done.1), channel_id=1, source_target_pairs={{0,1},{1,0},{2,3},{3,2},{4,5},{5,4},{6,7},{7,6},{8,9},{9,8},{10,11... | collective-permute-start | bytes 417800 | tf_op jit(solution)/shard_map/ppermute | solution.py:24
  39.3 4.1 %collective-permute-start.8 = (bf16[544,128]{1,0:T(8,128)(2,1)S(1)}, bf16[544,128]{1,0:T(8,128)(2,1)S(1)}, u32[]{:S(2)}, u32[]{:S(2)}) collective-permute-start(bf16[544,128]{1,0:T(8,128)(2,1)S(1)} %collective-permute-done.rest_1_), channel_id=1, source_target_pairs={{0,1},{1,0},{2,3},{3,2},{4,5},{5,4},{6,7},{7,6},{8,9},{9,8},{10,11... | collective-permute-start | bytes 417800 | tf_op jit(solution)/shard_map/ppermute | solution.py:24
  40.4 3.0 %collective-permute-start.9 = (bf16[544,128]{1,0:T(8,128)(2,1)S(1)}, bf16[544,128]{1,0:T(8,128)(2,1)S(1)}, u32[]{:S(2)}, u32[]{:S(2)}) collective-permute-start(bf16[544,128]{1,0:T(8,128)(2,1)S(1)} %collective-permute-done.1.rest_2_), channel_id=1, source_target_pairs={{0,1},{1,0},{2,3},{3,2},{4,5},{5,4},{6,7},{7,6},{8,9},{9,8},{10,11... | collective-permute-start | bytes 417800 | tf_op jit(solution)/shard_map/ppermute | solution.py:24
  40.4 3.7 %collective-permute-start.10 = (bf16[544,128]{1,0:T(8,128)(2,1)S(1)}, bf16[544,128]{1,0:T(8,128)(2,1)S(1)}, u32[]{:S(2)}, u32[]{:S(2)}) collective-permute-start(bf16[544,128]{1,0:T(8,128)(2,1)S(1)} %collective-permute-done.2.rest_3_), channel_id=1, source_target_pairs={{0,1},{1,0},{2,3},{3,2},{4,5},{5,4},{6,7},{7,6},{8,9},{9,8},{10,11... | collective-permute-start | bytes 417800 | tf_op jit(solution)/shard_map/ppermute | solution.py:24
  42.8 1.4 %collective-permute-start.11 = (bf16[544,128]{1,0:T(8,128)(2,1)S(1)}, bf16[544,128]{1,0:T(8,128)(2,1)S(1)}, u32[]{:S(2)}, u32[]{:S(2)}) collective-permute-start(bf16[544,128]{1,0:T(8,128)(2,1)S(1)} %collective-permute-done.3.rest_4_), channel_id=1, source_target_pairs={{0,1},{1,0},{2,3},{3,2},{4,5},{5,4},{6,7},{7,6},{8,9},{9,8},{10,11... | collective-permute-start | bytes 417800 | tf_op jit(solution)/shard_map/ppermute | solution.py:24
  42.9 1.6 %collective-permute-start.12 = (bf16[544,128]{1,0:T(8,128)(2,1)S(1)}, bf16[544,128]{1,0:T(8,128)(2,1)S(1)}, u32[]{:S(2)}, u32[]{:S(2)}) collective-permute-start(bf16[544,128]{1,0:T(8,128)(2,1)S(1)} %collective-permute-done.4.rest_5_), channel_id=1, source_target_pairs={{0,1},{1,0},{2,3},{3,2},{4,5},{5,4},{6,7},{7,6},{8,9},{9,8},{10,11... | collective-permute-start | bytes 417800 | tf_op jit(solution)/shard_map/ppermute | solution.py:24
  43.4 1.4 %collective-permute-start.13 = (bf16[544,128]{1,0:T(8,128)(2,1)S(1)}, bf16[544,128]{1,0:T(8,128)(2,1)S(1)}, u32[]{:S(2)}, u32[]{:S(2)}) collective-permute-start(bf16[544,128]{1,0:T(8,128)(2,1)S(1)} %collective-permute-done.5.rest_6_), channel_id=1, source_target_pairs={{0,1},{1,0},{2,3},{3,2},{4,5},{5,4},{6,7},{7,6},{8,9},{9,8},{10,11... | collective-permute-start | bytes 417800 | tf_op jit(solution)/shard_map/ppermute | solution.py:24
  43.5 1.5 %collective-permute-start.14 = (bf16[544,128]{1,0:T(8,128)(2,1)S(1)}, bf16[544,128]{1,0:T(8,128)(2,1)S(1)}, u32[]{:S(2)}, u32[]{:S(2)}) collective-permute-start(bf16[544,128]{1,0:T(8,128)(2,1)S(1)} %collective-permute-done.6.rest_7_), channel_id=1, source_target_pairs={{0,1},{1,0},{2,3},{3,2},{4,5},{5,4},{6,7},{7,6},{8,9},{9,8},{10,11... | collective-permute-start | bytes 417800 | tf_op jit(solution)/shard_map/ppermute | solution.py:24

commit v2 on v1

v2 whole, which is shorter than its diff:
```python
import math

import jax
import jax.numpy as jnp
from jax import lax
from jax.experimental import pallas as pl
from jax.experimental.pallas import tpu as pltpu
from jax.sharding import PartitionSpec as P

HEAD = 128
KV_HEADS = 8
SLOTS = 4
TOKENS = 256
KEYS = 256
DEVICES = 128
CHIP_MASKS = tuple((d >> 2) * 32 + (d >> 1 & 1) * 4 + (d & 1) * 2 for d in range(8))
ORDER = (0, 7, 6, 5, 3, 4, 2, 1)
EARLY = 4
AFTER = (0, 0, 0, 0, 0, 1, 2, 3)
PREPARE_FLOPS = 2850000000
PACK_LIMIT = 60
PIECE = 2 * KEYS + 32
CHUNKS = 17
BLOCK = 128
SCALE = math.log2(math.e) / math.sqrt(HEAD)
HIDDEN = -1e30


def swap(array, mask):
    return lax.ppermute(array, "ctx", [(i, i ^ mask) for i in range(DEVICES)])


def pack_kernel(head_ref, live_ref, *rest):
    given, send, pieces, tail, held, sems = rest[:5], rest[5], rest[6:14], rest[14], rest[15:20], rest[20]
    f32, bf16 = jnp.float32, jnp.bfloat16
    fetches = [pltpu.make_async_copy(given[i], held[i], sems.at[i]) for i in range(5)]
    for fetch in fetches:
        fetch.start()
    queries, new_keys, new_values, keys, values = held
    fetches[0].wait()
    for device in range(DEVICES):
        at = ((device >> 5 & 1) * 8 + (device >> 2 & 1) * 4 + (device & 3)) * 256
        send[device] = queries[:, at : at + 256]
    width = KV_HEADS * HEAD
    fetches[1].wait()
    fetches[2].wait()
    live = jnp.full((8, width), live_ref[0].astype(f32))
    gap = jnp.zeros((4, width), f32)
    tail[0:16, :] = jnp.concatenate([new_keys[...].astype(f32), gap, live], axis=0).astype(bf16)
    tail[16:32, :] = jnp.concatenate([new_values[...].astype(f32), gap, gap, gap], axis=0).astype(bf16)
    head = head_ref[0]
    columns = [pl.ds(pl.multiple_of((head ^ d) * HEAD, HEAD), HEAD) for d in range(8)]
    for d in range(8):
        pieces[d][2 * KEYS : PIECE, :] = tail[:, columns[d]]
    fetches[3].wait()
    for d in range(8):
        pieces[d][0:KEYS, :] = keys[:, columns[d]]
    fetches[4].wait()
    for d in range(8):
        pieces[d][KEYS : 2 * KEYS, :] = values[:, columns[d]]


def pack(head, live, queries, new_keys, new_values, keys, values):
    whole = pl.BlockSpec(memory_space=pltpu.VMEM)
    return pl.pallas_call(
        pack_kernel,
        out_shape=[jax.ShapeDtypeStruct((DEVICES, SLOTS, 256), jnp.bfloat16)]
        + [jax.ShapeDtypeStruct((PIECE, HEAD), jnp.bfloat16)] * 8,
        in_specs=[pl.BlockSpec(memory_space=pltpu.SMEM)] * 2
        + [pl.BlockSpec(memory_space=pl.ANY)] * 5,
        out_specs=[whole] * 9,
        scratch_shapes=[
            pltpu.VMEM((32, KV_HEADS * HEAD), jnp.bfloat16),
            pltpu.VMEM((SLOTS, 4096), jnp.bfloat16),
            pltpu.VMEM((SLOTS, KV_HEADS * HEAD), jnp.bfloat16),
            pltpu.VMEM((SLOTS, KV_HEADS * HEAD), jnp.bfloat16),
            pltpu.VMEM((KEYS, KV_HEADS * HEAD), jnp.bfloat16),
            pltpu.VMEM((KEYS, KV_HEADS * HEAD), jnp.bfloat16),
            pltpu.SemaphoreType.DMA((5,)),
        ],
        compiler_params=pltpu.CompilerParams(vmem_limit_bytes=PACK_LIMIT << 20),
        cost_estimate=pl.CostEstimate(flops=0, bytes_accessed=2 << 20, transcendentals=0),
        name="pack",
    )(head, live, queries, new_keys, new_values, keys, values)


def prepare_kernel(here_ref, col_ref, row_ref, *rest):
    pieces, (pick, near, far, token_ref, tails) = rest[:EARLY], rest[EARLY:]
    f32, bf16, i32 = jnp.float32, jnp.bfloat16, jnp.int32
    here = here_ref[0]
    iota = lambda shape, dim: lax.broadcasted_iota(i32, shape, dim)
    own_col, own_row = col_ref[...], row_ref[...]

    same = own_col == own_row
    down, across = iota((TOKENS, TOKENS), 0), iota((TOKENS, TOKENS), 1)
    rank_col = jnp.sum(jnp.where(same & (across < down), 1.0, 0.0), axis=1, keepdims=True)
    rank_row = jnp.sum(jnp.where(same & (down < across), 1.0, 0.0), axis=0, keepdims=True)
    place_col = own_col * SLOTS + rank_col.astype(i32)
    place_row = own_row * SLOTS + rank_row.astype(i32)

    pick[...] = jnp.where(place_col == iota((TOKENS, DEVICES * SLOTS), 1), 1.0, 0.0).astype(bf16)
    line = (down >> 1) * SLOTS + (down & 1)
    near[...] = jnp.where(line == place_row, 1.0, 0.0).astype(bf16)
    far[...] = jnp.where(line + 2 == place_row, 1.0, 0.0).astype(bf16)

    column = iota((1, KEYS), 1)
    part, row = column >> 4, column & 15
    chip = jnp.zeros_like(part)
    for number, d in enumerate(ORDER):
        chip = jnp.where((part & 7) == number, CHIP_MASKS[d], chip)
    device = here ^ (chip + (part >> 3))
    slot = jnp.where(row < SLOTS, device * SLOTS + row, -1)
    token = jnp.where(place_col == slot, down.astype(f32) + 1.0, 0.0)
    token_ref[...] = jnp.sum(token, axis=0, keepdims=True) - 1.0

    for p in range(EARLY):
        tails[32 * p : 32 * p + 32, :] = pieces[p][2 * KEYS : PIECE, :]


def prepare(here, own_col, own_row, pieces):
    whole = pl.BlockSpec(memory_space=pltpu.VMEM)
    shape = jax.ShapeDtypeStruct
    return pl.pallas_call(
        prepare_kernel,
        out_shape=[
            shape((TOKENS, DEVICES * SLOTS), jnp.bfloat16),
            shape((TOKENS, TOKENS), jnp.bfloat16),
            shape((TOKENS, TOKENS), jnp.bfloat16),
            shape((1, KEYS), jnp.float32),
            shape((32 * EARLY, HEAD), jnp.bfloat16),
        ],
        in_specs=[pl.BlockSpec(memory_space=pltpu.SMEM)] + [whole] * (2 + EARLY),
        out_specs=[whole] * 5,
        compiler_params=pltpu.CompilerParams(vmem_limit_bytes=8 << 20),
        cost_estimate=pl.CostEstimate(flops=PREPARE_FLOPS, bytes_accessed=1 << 19, transcendentals=0),
        name="prepare",
    )(here, own_col, own_row, *pieces)


def attend_kernel(q_ref, pick, near, far, token_ref, tails, *rest):
    pieces, out_ref = rest[:16], rest[16]
    scores, bias, new_keys, new_values = rest[17:]
    f32, bf16 = jnp.float32, jnp.bfloat16
    iota = lambda shape, dim: lax.broadcasted_iota(jnp.int32, shape, dim)

    by_token = jnp.dot(pick[...], q_ref[...], preferred_element_type=f32).astype(bf16)
    first_lane = jnp.where(iota((BLOCK, HEAD), 1) == 0, 1.0, 0.0).astype(bf16)

    key_row = iota((KEYS, HEAD), 0).astype(f32)
    for p in range(16):
        tail = pieces[p][2 * KEYS : PIECE, :] if p >= EARLY else tails[32 * p : 32 * p + 32, :]
        new_keys[16 * p : 16 * p + 16, :] = tail[0:16]
        new_values[16 * p : 16 * p + 16, :] = tail[16:32]
        live = tail[0:16].astype(f32)[8:9, 0:1]
        bias[p] = jnp.where(key_row < live, 0.0, HIDDEN).astype(bf16)

    token = token_ref[...]
    contract = (((1,), (1,)), ((), ()))
    lanes = iota((BLOCK, HEAD), 1)
    place = lanes & 63
    rows = []
    for b in range(4):
        head, start = b // 2, b % 2 * BLOCK
        plain = by_token[start : start + BLOCK, head * HEAD : (head + 1) * HEAD]
        query = jnp.concatenate([plain, first_lane], axis=1)
        peak = jnp.full((BLOCK, HEAD), HIDDEN, f32)
        for p in range(16):
            key = jnp.concatenate([pieces[p][0:KEYS, :], bias[p]], axis=1)
            score = lax.dot_general(query, key, contract, preferred_element_type=f32)
            scores[b, p] = score
            peak = jnp.maximum(peak, jnp.maximum(score[:, :HEAD], score[:, HEAD:]))
        reader = (iota((BLOCK, 1), 0) + start).astype(f32)
        seen = (token >= 0.0) & (token <= reader)
        score = lax.dot_general(plain, new_keys[...], contract, preferred_element_type=f32)
        score = jnp.where(seen, score, HIDDEN)
        scores[b, 16] = score
        peak = jnp.maximum(peak, jnp.maximum(score[:, :HEAD], score[:, HEAD:]))
        peak = jnp.max(peak, axis=1, keepdims=True)

        total = jnp.zeros((BLOCK, HEAD), f32)
        mixed = jnp.zeros((BLOCK, HEAD), f32)
        for p in range(CHUNKS):
            weight = jnp.exp2((scores[b, p] - peak) * SCALE)
            total = total + (weight[:, :HEAD] + weight[:, HEAD:])
            value = new_values[...] if p == 16 else pieces[p][KEYS : 2 * KEYS, :]
            mixed = mixed + jnp.dot(weight.astype(bf16), value, preferred_element_type=f32)
        total = jnp.sum(total, axis=1, keepdims=True)
        mean = mixed / total

        reach = jnp.max(jnp.abs(mean), axis=1, keepdims=True)
        step = jnp.round(jnp.log2(jnp.maximum(reach, 1e-30)))
        mean = mean * jnp.exp2(-step)
        rough = mean.astype(bf16)
        fine = (mean - rough.astype(f32)).astype(bf16)
        level = peak * SCALE + jnp.log2(total)
        high = level.astype(bf16).astype(f32)
        middle = (level - high).astype(bf16).astype(f32)
        low = level - high - middle
        parts = jnp.zeros((BLOCK, HEAD), f32)
        for number, value in enumerate((high, middle, low, step)):
            parts = jnp.where(place == 2 * number + head, value, parts)
        rows.append((rough, fine, parts))

    whole = jnp.concatenate(
        [
            jnp.concatenate([rows[h][0], rows[h + 2][0], rows[h][1], rows[h + 2][1], (rows[h][2] + rows[h + 2][2]).astype(bf16)], axis=1)
            for h in range(2)
        ],
        axis=0,
    )

    first = jnp.dot(near[...], whole, preferred_element_type=f32)
    second = jnp.dot(far[...], whole, preferred_element_type=f32)
    out_ref[:, 0:256] = first[:, 0:256] + first[:, 256:512]
    out_ref[:, 256:512] = second[:, 0:256] + second[:, 256:512]
    out_ref[:, 512:640] = jnp.where(iota((TOKENS, HEAD), 1) < 64, first[:, 512:], second[:, 512:])


def attend(queries, prepared, pieces):
    whole = pl.BlockSpec(memory_space=pltpu.VMEM)
    return pl.pallas_call(
        attend_kernel,
        out_shape=jax.ShapeDtypeStruct((TOKENS, 640), jnp.float32),
        in_specs=[whole] * 22,
        out_specs=whole,
        scratch_shapes=[
            pltpu.VMEM((4, CHUNKS, BLOCK, KEYS), jnp.float32),
            pltpu.VMEM((16, KEYS, HEAD), jnp.bfloat16),
            pltpu.VMEM((KEYS, HEAD), jnp.bfloat16),
            pltpu.VMEM((KEYS, HEAD), jnp.bfloat16),
        ],
        compiler_params=pltpu.CompilerParams(vmem_limit_bytes=20 << 20),
        cost_estimate=pl.CostEstimate(
            flops=4 * 512 * 4352 * 128, bytes_accessed=3 << 20, transcendentals=512 * 4352
        ),
        name="attend",
    )(queries, *prepared, *pieces)


def combine_kernel(parts_ref, out_ref, whole):
    split = lambda array: array.reshape(2, 2, 4, 8, 2, array.shape[-1])
    levels = parts_ref[:, :, 512:640]
    ahead = lambda count: pltpu.roll(levels, HEAD - count, 2)
    step = jnp.exp2(ahead(6))
    level = split(levels + ahead(2) + ahead(4))
    factor = jnp.exp2(level - jnp.max(level, axis=(0, 2), keepdims=True))
    factor = factor / jnp.sum(factor, axis=(0, 2), keepdims=True) * split(step)
    for v in range(4):
        at = 64 * (v // 2) + v % 2
        mean = split(parts_ref[:, :, v * HEAD : (v + 1) * HEAD])
        mean = jnp.sum(mean * factor[..., at : at + 1], axis=(0, 2)).reshape(16, 2, HEAD)
        for pair in range(16):
            column = pair * 256 + v % 2 * HEAD
            whole[v // 2 * 2 : v // 2 * 2 + 2, column : column + HEAD] = mean[pair]
    out_ref[...] = whole[...].astype(jnp.bfloat16)


def combine(parts):
    whole = pl.BlockSpec(memory_space=pltpu.VMEM)
    return pl.pallas_call(
        combine_kernel,
        out_shape=jax.ShapeDtypeStruct((SLOTS, 4096), jnp.bfloat16),
        in_specs=[whole],
        out_specs=whole,
        scratch_shapes=[pltpu.VMEM((SLOTS, 4096), jnp.float32)],
        compiler_params=pltpu.CompilerParams(vmem_limit_bytes=16 << 20),
        name="combine",
    )(parts)


def per_device(queries, owners, new_keys, new_values, cache_keys, cache_values, lengths):
    bf16 = jnp.bfloat16
    here = lax.axis_index("ctx").astype(jnp.int32)
    head = (here >> 5 & 1) * 4 + (here >> 2 & 1) * 2 + (here >> 1 & 1)

    send, *mine = pack(head[None], lengths, queries, new_keys, new_values, cache_keys, cache_values)
    held = [mine[0]]
    for number, d in enumerate(ORDER[1:], 1):
        piece = mine[d]
        if AFTER[number]:
            piece, _ = lax.optimization_barrier((piece, held[AFTER[number]]))
        held.append(swap(piece, CHIP_MASKS[d]))
    other = [swap(piece, 1) for piece in held]
    everyone = lax.all_to_all(send, "ctx", 0, 0).reshape(DEVICES * SLOTS, 256)
    prepared = prepare(here[None], owners, owners.reshape(1, TOKENS), held[:EARLY])
    partial = attend(everyone, prepared, held + other)
    partial = partial.astype(jnp.float16).reshape(DEVICES, 2, 640)
    return combine(lax.all_to_all(partial, "ctx", 0, 0).astype(jnp.float32))


def solution(mesh):
    return jax.shard_map(
        per_device,
        mesh=mesh,
        in_specs=(
            P(("batch", "ctx"), None),
            P("batch", None),
            P(("batch", "ctx"), None),
            P(("batch", "ctx"), None),
            P(("batch", "ctx"), None),
            P(("batch", "ctx"), None),
            P(("batch", "ctx")),
        ),
        out_specs=P(("batch", "ctx"), None),
        check_vma=False,
    )
```

time: 82.9 us -> 71.6 us (0.86)
  starting transfers between devices: 39.1 us -> 29.6 us
  waiting for transfers between devices: 2.47 us -> 5.58 us
  local copies, waits for them, and re-layouts: 2.34 us -> 0.37 us
  Pallas kernels: 11.6 us -> 10.3 us
  other arithmetic: 1.11 us -> 0.27 us
    ppermute x15, starting transfers between devices: 24.1 us -> 18.1 us  [swap(): return lax.ppermute(array, 'ctx', [(i, i ^ mask) for i in range(DEVICES)])]
    all_to_all x1, starting transfers between devices: 15 us -> 11.5 us  [per_device(): everyone = lax.all_to_all(send, 'ctx', 0, 0).reshape(DEVICES * SLOTS, 256)]
    all_to_all x1, waiting for transfers between devices: 0.01 us -> 2.56 us  [per_device(): everyone = lax.all_to_all(send, 'ctx', 0, 0).reshape(DEVICES * SLOTS, 256)]
    pallas_call x1, Pallas kernels: 7.09 us -> 5.64 us  [attend(): pl.pallas_call(attend_kernel, out_shape=jax.ShapeDtypeStruct((TOKENS, 640...]
    reshape x2 -> x1, local copies, waits for them, and re-layouts: 1.47 us -> 0.16 us  [per_device(): partial = partial.astype(jnp.float16).reshape(DEVICES, 2, 640)]
    pallas_call x1 -> x2, Pallas kernels: 2.07 us -> 2.15 us  [the longest x1 1.8 us: combine(): pl.pallas_call(combine_kernel, out_shape=jax.ShapeDtypeStruct((SLOTS, 409...]
  transfers between devices with their start and end apart: 16 -> 16, of which waited for: 6 -> 3; matrix products, arithmetic and copies ran while one was open for 0% -> 0% of each run, Pallas kernels for 0% -> 0%
where the time goes in v2:
time: 71.6 us; the launch traced here: 71.4 us
  starting transfers between devices  29.6 us (41%)
  blocking collectives  24.4 us (34%)
  Pallas kernels  10.3 us (14%)
  waiting for transfers between devices  5.58 us (8%)
  between operations  0.78 us (1%)
    all_to_all x1, blocking collectives, per_device(): return combine(lax.all_to_all(partial, 'ctx', 0, 0).astype(jnp.float32))  24.4 us
    ppermute x15, starting transfers between devices, swap(): return lax.ppermute(array, 'ctx', [(i, i ^ mask) for i in range(DEVICES)])  18.1 us
    all_to_all x1, starting transfers between devices, per_device(): everyone = lax.all_to_all(send, 'ctx', 0, 0).reshape(DEVICES * SLOTS, 256)  11.5 us
    pallas_call x1, Pallas kernels, attend(): pl.pallas_call(attend_kernel, out_shape=jax.ShapeDtypeStruct((TOKENS, 640...  5.64 us
    ppermute x15, waiting for transfers between devices, swap(): return lax.ppermute(array, 'ctx', [(i, i ^ mask) for i in range(DEVICES)])  3.03 us
    all_to_all x1, waiting for transfers between devices, per_device(): everyone = lax.all_to_all(send, 'ctx', 0, 0).reshape(DEVICES * SLOTS, 256)  2.56 us
    pallas_call x1, Pallas kernels, pack(): pl.pallas_call(pack_kernel, out_shape=[jax.ShapeDtypeStruct((DEVICES, SLO...  2.54 us
    pallas_call x1, Pallas kernels, combine(): pl.pallas_call(combine_kernel, out_shape=jax.ShapeDtypeStruct((SLOTS, 409...  1.8 us
  transfers between devices with their start and end apart: 16, of which 3 were waited for; matrix products, arithmetic and copies ran while one was open for 0% of the time, Pallas kernels for 0%

profile of v2, /device:TPU:1, one launch (start us, length us, event | category | flops | bytes accessed | tf_op | source)
XLA Modules:
  0.0 71.4 jit_solution(9124415300988253554)
XLA Ops:
  0.7 2.5 %pack.1 = (bf16[128,4,256]{2,1,0:T(4,128)(2,1)}, bf16[544,128]{1,0:T(8,128)(2,1)}, bf16[544,128]{1,0:T(8,128)(2,1)}, bf16[544,128]{1,0:T(8,128)(2,1)}, bf16[544,...) custom-call(s32[1]{0:T(128)} %bitcast.head_ref, ...), custom_call_target="tpu_custom_call" | custom-call | bytes 2097152 | tf_op jit(solution)/shard_map/pack/pallas_call | solution.py:65
  3.2 4.5 %collective-permute-start = (bf16[544,128]{1,0:T(8,128)(2,1)}, bf16[544,128]{1,0:T(8,128)(2,1)S(1)}, u32[]{:S(2)}, u32[]{:S(2)}) collective-permute-start(bf16[544,128]{1,0:T(8,128)(2,1)} %get-tuple-element.24), channel_id=1, source_target_pairs={{0,38},{1,39},{2,36},{3,37},{4,34},{5,35},{6,32},{7,33},{8,46},{9,... | collective-permute-start | bytes 417800 | tf_op jit(solution)/shard_map/ppermute | solution.py:30
  7.7 1.0 %collective-permute-start.2 = (bf16[544,128]{1,0:T(8,128)(2,1)}, bf16[544,128]{1,0:T(8,128)(2,1)S(1)}, u32[]{:S(2)}, u32[]{:S(2)}) collective-permute-start(bf16[544,128]{1,0:T(8,128)(2,1)} %get-tuple-element.26), channel_id=1, source_target_pairs={{0,34},{1,35},{2,32},{3,33},{4,38},{5,39},{6,36},{7,37},{8,42},{9,... | collective-permute-start | bytes 417800 | tf_op jit(solution)/shard_map/ppermute | solution.py:30
  8.7 2.6 %collective-permute-start.3 = (bf16[544,128]{1,0:T(8,128)(2,1)}, bf16[544,128]{1,0:T(8,128)(2,1)S(1)}, u32[]{:S(2)}, u32[]{:S(2)}) collective-permute-start(bf16[544,128]{1,0:T(8,128)(2,1)} %get-tuple-element.32), channel_id=1, source_target_pairs={{0,6},{1,7},{2,4},{3,5},{4,2},{5,3},{6,0},{7,1},{8,14},{9,15},{10,... | collective-permute-start | bytes 417800 | tf_op jit(solution)/shard_map/ppermute | solution.py:30
  11.2 1.8 %collective-permute-start.7 = (bf16[544,128]{1,0:T(8,128)(2,1)}, bf16[544,128]{1,0:T(8,128)(2,1)S(1)}, u32[]{:S(2)}, u32[]{:S(2)}) collective-permute-start(bf16[544,128]{1,0:T(8,128)(2,1)} %get-tuple-element.23.rest_0_), channel_id=1, source_target_pairs={{0,1},{1,0},{2,3},{3,2},{4,5},{5,4},{6,7},{7,6},{8,9},{9,8},{10,11... | collective-permute-start | bytes 417800 | tf_op jit(solution)/shard_map/ppermute | solution.py:30
  13.0 11.5 %all-to-all-start = ((bf16[128,4,256]{2,1,0:T(4,128)(2,1)}), bf16[128,4,256]{2,1,0:T(4,128)(2,1)S(1)}, u32[]{:S(2)}, u32[]{:S(2)}) async-start(bf16[128,4,256]{2,1,0:T(4,128)(2,1)} %get-tuple-element.22), calls=%async_computation | async-start | bytes 524288 | tf_op jit(solution)/shard_map/all_to_all | solution.py:284
  24.6 1.6 %collective-permute-start.4 = (bf16[544,128]{1,0:T(8,128)(2,1)}, bf16[544,128]{1,0:T(8,128)(2,1)S(1)}, u32[]{:S(2)}, u32[]{:S(2)}) collective-permute-start(bf16[544,128]{1,0:T(8,128)(2,1)} %get-tuple-element.34), channel_id=1, source_target_pairs={{0,32},{1,33},{2,34},{3,35},{4,36},{5,37},{6,38},{7,39},{8,40},{9,... | collective-permute-start | bytes 417800 | tf_op jit(solution)/shard_map/ppermute | solution.py:30
  26.1 0.0 collective-permute-done.1.rest_2_
  26.1 1.3 %collective-permute-start.5 = (bf16[544,128]{1,0:T(8,128)(2,1)S(1)}, bf16[544,128]{1,0:T(8,128)(2,1)S(1)}, u32[]{:S(2)}, u32[]{:S(2)}) collective-permute-start(bf16[544,128]{1,0:T(8,128)(2,1)S(1)} %copy-done.3), channel_id=1, source_target_pairs={{0,4},{1,5},{2,6},{3,7},{4,0},{5,1},{6,2},{7,3},{8,12},{9,13},{10,... | collective-permute-start | bytes 417800 | tf_op jit(solution)/shard_map/ppermute | solution.py:30
  27.4 0.0 collective-permute-done.2.rest_3_
  27.4 0.9 %collective-permute-start.8 = (bf16[544,128]{1,0:T(8,128)(2,1)S(1)}, bf16[544,128]{1,0:T(8,128)(2,1)S(1)}, u32[]{:S(2)}, u32[]{:S(2)}) collective-permute-start(bf16[544,128]{1,0:T(8,128)(2,1)S(1)} %collective-permute-done.rest_1_), channel_id=1, source_target_pairs={{0,1},{1,0},{2,3},{3,2},{4,5},{5,4},{6,7},{7,6},{8,9},{9,8},{10,11... | collective-permute-start | bytes 417800 | tf_op jit(solution)/shard_map/ppermute | solution.py:30
  28.4 0.1 collective-permute-start.9
  28.5 1.2 %collective-permute-start.6 = (bf16[544,128]{1,0:T(8,128)(2,1)S(1)}, bf16[544,128]{1,0:T(8,128)(2,1)S(1)}, u32[]{:S(2)}, u32[]{:S(2)}) collective-permute-start(bf16[544,128]{1,0:T(8,128)(2,1)S(1)} %copy-done.2), channel_id=1, source_target_pairs={{0,2},{1,3},{2,0},{3,1},{4,6},{5,7},{6,4},{7,5},{8,10},{9,11},{10,... | collective-permute-start | bytes 417800 | tf_op jit(solution)/shard_map/ppermute | solution.py:30
  29.7 0.1 copy.8.col_ref
  29.8 0.7 %collective-permute-done.4.rest_5_ = bf16[544,128]{1,0:T(8,128)(2,1)S(1)} collective-permute-done((bf16[544,128]{1,0:T(8,128)(2,1)}, bf16[544,128]{1,0:T(8,128)(2,1)S(1)}, u32[]{:S(2)}, u32[]{:S(2)}) %collective-permute-start.4) | collective-permute-done | bytes 139296 | tf_op jit(solution)/shard_map/ppermute | solution.py:30
  30.5 1.8 %collective-permute-start.10 = (bf16[544,128]{1,0:T(8,128)(2,1)S(1)}, bf16[544,128]{1,0:T(8,128)(2,1)S(1)}, u32[]{:S(2)}, u32[]{:S(2)}) collective-permute-start(bf16[544,128]{1,0:T(8,128)(2,1)S(1)} %collective-permute-done.2.rest_3_), channel_id=1, source_target_pairs={{0,1},{1,0},{2,3},{3,2},{4,5},{5,4},{6,7},{7,6},{8,9},{9,8},{10,11... | collective-permute-start | bytes 417800 | tf_op jit(solution)/shard_map/ppermute | solution.py:30
  32.4 0.0 collective-permute-start.11
  32.4 2.3 %collective-permute-done.5.rest_6_ = bf16[544,128]{1,0:T(8,128)(2,1)S(1)} collective-permute-done((bf16[544,128]{1,0:T(8,128)(2,1)S(1)}, bf16[544,128]{1,0:T(8,128)(2,1)S(1)}, u32[]{:S(2)}, u32[]{:S(2)}) %collective-permute-start.5) | collective-permute-done | bytes 139296 | tf_op jit(solution)/shard_map/ppermute | solution.py:30
  34.6 0.9 %collective-permute-start.12 = (bf16[544,128]{1,0:T(8,128)(2,1)S(1)}, bf16[544,128]{1,0:T(8,128)(2,1)S(1)}, u32[]{:S(2)}, u32[]{:S(2)}) collective-permute-start(bf16[544,128]{1,0:T(8,128)(2,1)S(1)} %collective-permute-done.4.rest_5_), channel_id=1, source_target_pairs={{0,1},{1,0},{2,3},{3,2},{4,5},{5,4},{6,7},{7,6},{8,9},{9,8},{10,11... | collective-permute-start | bytes 417800 | tf_op jit(solution)/shard_map/ppermute | solution.py:30
  35.5 0.0 collective-permute-done.9.rest_10_
  35.5 0.0 collective-permute-start.13
  35.5 0.0 collective-permute-done.6.rest_7_
  35.5 0.5 collective-permute-start.14
  36.0 0.4 prepare.1
  36.4 2.6 %all-to-all-done = bf16[128,4,256]{2,1,0:T(4,128)(2,1)S(1)} async-done(((bf16[128,4,256]{2,1,0:T(4,128)(2,1)}), bf16[128,4,256]{2,1,0:T(4,128)(2,1)S(1)}, u32[]{:S(2)}, u32[]{:S(2)}) %all-to-all-start) | async-done | bytes 262176 | tf_op jit(solution)/shard_map/all_to_all | solution.py:284
  38.9 0.1 reshape.9.q_ref
  39.0 0.0 collective-permute-done.11.rest_12_
  39.1 5.6 %attend.1 = f32[256,640]{1,0:T(8,128)S(1)} custom-call(bf16[512,256]{1,0:T(8,128)(2,1)S(1)} %reshape.9.q_ref, bf16[256,512]{1,0:T(8,128)(2,1)S(1)} %get-tuple-element.27.pick, bf16[256,256]{1,0:T(8,128)(2,1)S(1)} %get-tuple-element.28.near, bf16[256,256]{1,0:T(8,128)(2,1)S(1)} %get-tuple-element.29.far, f32[1,256]{1,0:T(1,128)S(1)} %get-tuple-element.30.token_ref, ...), custom_call_target="tpu_custom_call" | custom-call | flops 1140850688 | bytes 3145728 | tf_op jit(solution)/shard_map/attend/pallas_call | solution.py:221
  44.8 0.2 reshape.11
  44.9 24.4 %all_to_all.10 = f16[128,2,640]{2,1,0:T(2,128)(2,1)S(1)} all-to-all(f16[128,2,640]{2,1,0:T(2,128)(2,1)S(1)} %reshape.11), channel_id=1, replica_groups=mesh['batch'=2,'ctx'=128] {'ctx'}, dimensions={0} | all-to-all | bytes 655360 | tf_op jit(solution)/shard_map/all_to_all | solution.py:288
  69.3 0.2 convert_element_type.7.parts_ref
  69.6 1.8 %combine.1 = bf16[4,4096]{1,0:T(4,128)(2,1)} custom-call(f32[128,2,640]{2,1,0:T(2,128)S(1)} %convert_element_type.7.parts_ref), custom_call_target="tpu_custom_call" | custom-call | tf_op jit(solution)/shard_map/combine/pallas_call | solution.py:260
  (18 shorter events, 0.1 us)
Async XLA Ops:
  3.2 21.3 %collective-permute-start = (bf16[544,128]{1,0:T(8,128)(2,1)}, bf16[544,128]{1,0:T(8,128)(2,1)S(1)}, u32[]{:S(2)}, u32[]{:S(2)}) collective-permute-start(bf16[544,128]{1,0:T(8,128)(2,1)} %get-tuple-element.24), channel_id=1, source_target_pairs={{0,38},{1,39},{2,36},{3,37},{4,34},{5,35},{6,32},{7,33},{8,46},{9,... | collective-permute-start | bytes 417800 | tf_op jit(solution)/shard_map/ppermute | solution.py:30
  7.7 18.4 %collective-permute-start.1 = (bf16[544,128]{1,0:T(8,128)(2,1)}, bf16[544,128]{1,0:T(8,128)(2,1)S(1)}, u32[]{:S(2)}, u32[]{:S(2)}) collective-permute-start(bf16[544,128]{1,0:T(8,128)(2,1)} %get-tuple-element.25), channel_id=1, source_target_pairs={{0,36},{1,37},{2,38},{3,39},{4,32},{5,33},{6,34},{7,35},{8,44},{9,... | collective-permute-start | bytes 417800 | tf_op jit(solution)/shard_map/ppermute | solution.py:30
  7.7 19.7 %collective-permute-start.2 = (bf16[544,128]{1,0:T(8,128)(2,1)}, bf16[544,128]{1,0:T(8,128)(2,1)S(1)}, u32[]{:S(2)}, u32[]{:S(2)}) collective-permute-start(bf16[544,128]{1,0:T(8,128)(2,1)} %get-tuple-element.26), channel_id=1, source_target_pairs={{0,34},{1,35},{2,32},{3,33},{4,38},{5,39},{6,36},{7,37},{8,42},{9,... | collective-permute-start | bytes 417800 | tf_op jit(solution)/shard_map/ppermute | solution.py:30
  8.7 19.7 %collective-permute-start.3 = (bf16[544,128]{1,0:T(8,128)(2,1)}, bf16[544,128]{1,0:T(8,128)(2,1)S(1)}, u32[]{:S(2)}, u32[]{:S(2)}) collective-permute-start(bf16[544,128]{1,0:T(8,128)(2,1)} %get-tuple-element.32), channel_id=1, source_target_pairs={{0,6},{1,7},{2,4},{3,5},{4,2},{5,3},{6,0},{7,1},{8,14},{9,15},{10,... | collective-permute-start | bytes 417800 | tf_op jit(solution)/shard_map/ppermute | solution.py:30
  11.2 17.2 %collective-permute-start.7 = (bf16[544,128]{1,0:T(8,128)(2,1)}, bf16[544,128]{1,0:T(8,128)(2,1)S(1)}, u32[]{:S(2)}, u32[]{:S(2)}) collective-permute-start(bf16[544,128]{1,0:T(8,128)(2,1)} %get-tuple-element.23.rest_0_), channel_id=1, source_target_pairs={{0,1},{1,0},{2,3},{3,2},{4,5},{5,4},{6,7},{7,6},{8,9},{9,8},{10,11... | collective-permute-start | bytes 417800 | tf_op jit(solution)/shard_map/ppermute | solution.py:30
  13.0 13.1 %copy-start.3 = (bf16[544,128]{1,0:T(8,128)(2,1)S(1)}, bf16[544,128]{1,0:T(8,128)(2,1)}, u32[]{:S(2)}) copy-start(bf16[544,128]{1,0:T(8,128)(2,1)} %get-tuple-element.36) | copy-start | bytes 417796
  13.0 15.4 %copy-start.2 = (bf16[544,128]{1,0:T(8,128)(2,1)S(1)}, bf16[544,128]{1,0:T(8,128)(2,1)}, u32[]{:S(2)}) copy-start(bf16[544,128]{1,0:T(8,128)(2,1)} %get-tuple-element.38) | copy-start | bytes 417796
  13.0 23.0 %copy-start.1 = (bf16[544,128]{1,0:T(8,128)(2,1)S(1)}, bf16[544,128]{1,0:T(8,128)(2,1)}, u32[]{:S(2)}) copy-start(bf16[544,128]{1,0:T(8,128)(2,1)} %get-tuple-element.23.rest_0_) | copy-start | bytes 417796
  13.0 25.9 %all-to-all-start = ((bf16[128,4,256]{2,1,0:T(4,128)(2,1)}), bf16[128,4,256]{2,1,0:T(4,128)(2,1)S(1)}, u32[]{:S(2)}, u32[]{:S(2)}) async-start(bf16[128,4,256]{2,1,0:T(4,128)(2,1)} %get-tuple-element.22), calls=%async_computation | async-start | bytes 524288 | tf_op jit(solution)/shard_map/all_to_all | solution.py:284
  24.6 6.0 %collective-permute-start.4 = (bf16[544,128]{1,0:T(8,128)(2,1)}, bf16[544,128]{1,0:T(8,128)(2,1)S(1)}, u32[]{:S(2)}, u32[]{:S(2)}) collective-permute-start(bf16[544,128]{1,0:T(8,128)(2,1)} %get-tuple-element.34), channel_id=1, source_target_pairs={{0,32},{1,33},{2,34},{3,35},{4,36},{5,37},{6,38},{7,39},{8,40},{9,... | collective-permute-start | bytes 417800 | tf_op jit(solution)/shard_map/ppermute | solution.py:30
  26.1 3.5 %copy-start = (s32[256,1]{0,1:T(1,128)S(1)}, s32[256,1]{0,1:T(1,128)}, u32[]{:S(2)}) copy-start(s32[256,1]{0,1:T(1,128)} %param.8) | copy-start | bytes 3076
  26.1 8.5 %collective-permute-start.5 = (bf16[544,128]{1,0:T(8,128)(2,1)S(1)}, bf16[544,128]{1,0:T(8,128)(2,1)S(1)}, u32[]{:S(2)}, u32[]{:S(2)}) collective-permute-start(bf16[544,128]{1,0:T(8,128)(2,1)S(1)} %copy-done.3), channel_id=1, source_target_pairs={{0,4},{1,5},{2,6},{3,7},{4,0},{5,1},{6,2},{7,3},{8,12},{9,13},{10,... | collective-permute-start | bytes 417800 | tf_op jit(solution)/shard_map/ppermute | solution.py:30
  27.4 4.9 %collective-permute-start.8 = (bf16[544,128]{1,0:T(8,128)(2,1)S(1)}, bf16[544,128]{1,0:T(8,128)(2,1)S(1)}, u32[]{:S(2)}, u32[]{:S(2)}) collective-permute-start(bf16[544,128]{1,0:T(8,128)(2,1)S(1)} %collective-permute-done.rest_1_), channel_id=1, source_target_pairs={{0,1},{1,0},{2,3},{3,2},{4,5},{5,4},{6,7},{7,6},{8,9},{9,8},{10,11... | collective-permute-start | bytes 417800 | tf_op jit(solution)/shard_map/ppermute | solution.py:30
  28.4 7.2 %collective-permute-start.9 = (bf16[544,128]{1,0:T(8,128)(2,1)S(1)}, bf16[544,128]{1,0:T(8,128)(2,1)S(1)}, u32[]{:S(2)}, u32[]{:S(2)}) collective-permute-start(bf16[544,128]{1,0:T(8,128)(2,1)S(1)} %collective-permute-done.1.rest_2_), channel_id=1, source_target_pairs={{0,1},{1,0},{2,3},{3,2},{4,5},{5,4},{6,7},{7,6},{8,9},{9,8},{10,11... | collective-permute-start | bytes 417800 | tf_op jit(solution)/shard_map/ppermute | solution.py:30
  28.5 7.1 %collective-permute-start.6 = (bf16[544,128]{1,0:T(8,128)(2,1)S(1)}, bf16[544,128]{1,0:T(8,128)(2,1)S(1)}, u32[]{:S(2)}, u32[]{:S(2)}) collective-permute-start(bf16[544,128]{1,0:T(8,128)(2,1)S(1)} %copy-done.2), channel_id=1, source_target_pairs={{0,2},{1,3},{2,0},{3,1},{4,6},{5,7},{6,4},{7,5},{8,10},{9,11},{10,... | collective-permute-start | bytes 417800 | tf_op jit(solution)/shard_map/ppermute | solution.py:30
  30.5 8.5 %collective-permute-start.10 = (bf16[544,128]{1,0:T(8,128)(2,1)S(1)}, bf16[544,128]{1,0:T(8,128)(2,1)S(1)}, u32[]{:S(2)}, u32[]{:S(2)}) collective-permute-start(bf16[544,128]{1,0:T(8,128)(2,1)S(1)} %collective-permute-done.2.rest_3_), channel_id=1, source_target_pairs={{0,1},{1,0},{2,3},{3,2},{4,5},{5,4},{6,7},{7,6},{8,9},{9,8},{10,11... | collective-permute-start | bytes 417800 | tf_op jit(solution)/shard_map/ppermute | solution.py:30
  32.4 6.7 %collective-permute-start.11 = (bf16[544,128]{1,0:T(8,128)(2,1)S(1)}, bf16[544,128]{1,0:T(8,128)(2,1)S(1)}, u32[]{:S(2)}, u32[]{:S(2)}) collective-permute-start(bf16[544,128]{1,0:T(8,128)(2,1)S(1)} %collective-permute-done.3.rest_4_), channel_id=1, source_target_pairs={{0,1},{1,0},{2,3},{3,2},{4,5},{5,4},{6,7},{7,6},{8,9},{9,8},{10,11... | collective-permute-start | bytes 417800 | tf_op jit(solution)/shard_map/ppermute | solution.py:30
  34.6 4.4 %collective-permute-start.12 = (bf16[544,128]{1,0:T(8,128)(2,1)S(1)}, bf16[544,128]{1,0:T(8,128)(2,1)S(1)}, u32[]{:S(2)}, u32[]{:S(2)}) collective-permute-start(bf16[544,128]{1,0:T(8,128)(2,1)S(1)} %collective-permute-done.4.rest_5_), channel_id=1, source_target_pairs={{0,1},{1,0},{2,3},{3,2},{4,5},{5,4},{6,7},{7,6},{8,9},{9,8},{10,11... | collective-permute-start | bytes 417800 | tf_op jit(solution)/shard_map/ppermute | solution.py:30
  35.5 3.5 %collective-permute-start.13 = (bf16[544,128]{1,0:T(8,128)(2,1)S(1)}, bf16[544,128]{1,0:T(8,128)(2,1)S(1)}, u32[]{:S(2)}, u32[]{:S(2)}) collective-permute-start(bf16[544,128]{1,0:T(8,128)(2,1)S(1)} %collective-permute-done.5.rest_6_), channel_id=1, source_target_pairs={{0,1},{1,0},{2,3},{3,2},{4,5},{5,4},{6,7},{7,6},{8,9},{9,8},{10,11... | collective-permute-start | bytes 417800 | tf_op jit(solution)/shard_map/ppermute | solution.py:30
  35.5 3.5 %collective-permute-start.14 = (bf16[544,128]{1,0:T(8,128)(2,1)S(1)}, bf16[544,128]{1,0:T(8,128)(2,1)S(1)}, u32[]{:S(2)}, u32[]{:S(2)}) collective-permute-start(bf16[544,128]{1,0:T(8,128)(2,1)S(1)} %collective-permute-done.6.rest_7_), channel_id=1, source_target_pairs={{0,1},{1,0},{2,3},{3,2},{4,5},{5,4},{6,7},{7,6},{8,9},{9,8},{10,11... | collective-permute-start | bytes 417800 | tf_op jit(solution)/shard_map/ppermute | solution.py:30

commit v3 on v2

--- a/solution.py
+++ b/solution.py
@@ -14,14 +14,14 @@
 KEYS = 256
 DEVICES = 128
 CHIP_MASKS = tuple((d >> 2) * 32 + (d >> 1 & 1) * 4 + (d & 1) * 2 for d in range(8))
-ORDER = (0, 7, 6, 5, 3, 4, 2, 1)
+ORDER = (0, 6, 5, 7, 3, 1, 4, 2)
 EARLY = 4
-AFTER = (0, 0, 0, 0, 0, 1, 2, 3)
+AFTER = (0, 0, 0, 0, 0, 2, 3, 4)
 PREPARE_FLOPS = 2850000000
 PACK_LIMIT = 60
 PIECE = 2 * KEYS + 32
 CHUNKS = 17
-BLOCK = 128
+BLOCK = 256
 SCALE = math.log2(math.e) / math.sqrt(HEAD)
 HIDDEN = -1e30
 
@@ -67,7 +67,7 @@
         out_shape=[jax.ShapeDtypeStruct((DEVICES, SLOTS, 256), jnp.bfloat16)]
         + [jax.ShapeDtypeStruct((PIECE, HEAD), jnp.bfloat16)] * 8,
         in_specs=[pl.BlockSpec(memory_space=pltpu.SMEM)] * 2
-        + [pl.BlockSpec(memory_space=pl.ANY)] * 5,
+        + [pl.BlockSpec(memory_space=pltpu.HBM)] * 5,
         out_specs=[whole] * 9,
         scratch_shapes=[
             pltpu.VMEM((32, KV_HEADS * HEAD), jnp.bfloat16),
@@ -139,34 +139,32 @@
 
 def attend_kernel(q_ref, pick, near, far, token_ref, tails, *rest):
     pieces, out_ref = rest[:16], rest[16]
-    scores, bias, new_keys, new_values = rest[17:]
+    scores, new_keys, new_values = rest[17:]
     f32, bf16 = jnp.float32, jnp.bfloat16
     iota = lambda shape, dim: lax.broadcasted_iota(jnp.int32, shape, dim)
 
     by_token = jnp.dot(pick[...], q_ref[...], preferred_element_type=f32).astype(bf16)
-    first_lane = jnp.where(iota((BLOCK, HEAD), 1) == 0, 1.0, 0.0).astype(bf16)
-
-    key_row = iota((KEYS, HEAD), 0).astype(f32)
+
+    lane_bias = []
     for p in range(16):
         tail = pieces[p][2 * KEYS : PIECE, :] if p >= EARLY else tails[32 * p : 32 * p + 32, :]
         new_keys[16 * p : 16 * p + 16, :] = tail[0:16]
         new_values[16 * p : 16 * p + 16, :] = tail[16:32]
         live = tail[0:16].astype(f32)[8:9, 0:1]
-        bias[p] = jnp.where(key_row < live, 0.0, HIDDEN).astype(bf16)
+        lane_bias.append(jnp.where(iota((1, KEYS), 1).astype(f32) < live, 0.0, HIDDEN))
 
     token = token_ref[...]
     contract = (((1,), (1,)), ((), ()))
-    lanes = iota((BLOCK, HEAD), 1)
-    place = lanes & 63
-    rows = []
-    for b in range(4):
-        head, start = b // 2, b % 2 * BLOCK
+    peaks = []
+    for b in range(2):
+        head, start = b, 0
         plain = by_token[start : start + BLOCK, head * HEAD : (head + 1) * HEAD]
-        query = jnp.concatenate([plain, first_lane], axis=1)
         peak = jnp.full((BLOCK, HEAD), HIDDEN, f32)
         for p in range(16):
-            key = jnp.concatenate([pieces[p][0:KEYS, :], bias[p]], axis=1)
-            score = lax.dot_general(query, key, contract, preferred_element_type=f32)
+            score = lax.dot_general(
+                plain, pieces[p][0:KEYS, :], contract, preferred_element_type=f32
+            )
+            score = score + lane_bias[p]
             scores[b, p] = score
             peak = jnp.maximum(peak, jnp.maximum(score[:, :HEAD], score[:, HEAD:]))
         reader = (iota((BLOCK, 1), 0) + start).astype(f32)
@@ -175,38 +173,38 @@
         score = jnp.where(seen, score, HIDDEN)
         scores[b, 16] = score
         peak = jnp.maximum(peak, jnp.maximum(score[:, :HEAD], score[:, HEAD:]))
-        peak = jnp.max(peak, axis=1, keepdims=True)
-
+        peaks.append(jnp.max(peak, axis=1, keepdims=True))
+
+    totals, sums = [], []
+    for b in range(2):
         total = jnp.zeros((BLOCK, HEAD), f32)
         mixed = jnp.zeros((BLOCK, HEAD), f32)
         for p in range(CHUNKS):
-            weight = jnp.exp2((scores[b, p] - peak) * SCALE)
+            weight = jnp.exp2((scores[b, p] - peaks[b]) * SCALE)
             total = total + (weight[:, :HEAD] + weight[:, HEAD:])
             value = new_values[...] if p == 16 else pieces[p][KEYS : 2 * KEYS, :]
             mixed = mixed + jnp.dot(weight.astype(bf16), value, preferred_element_type=f32)
-        total = jnp.sum(total, axis=1, keepdims=True)
-        mean = mixed / total
-
-        reach = jnp.max(jnp.abs(mean), axis=1, keepdims=True)
-        step = jnp.round(jnp.log2(jnp.maximum(reach, 1e-30)))
-        mean = mean * jnp.exp2(-step)
-        rough = mean.astype(bf16)
-        fine = (mean - rough.astype(f32)).astype(bf16)
-        level = peak * SCALE + jnp.log2(total)
-        high = level.astype(bf16).astype(f32)
-        middle = (level - high).astype(bf16).astype(f32)
-        low = level - high - middle
-        parts = jnp.zeros((BLOCK, HEAD), f32)
-        for number, value in enumerate((high, middle, low, step)):
-            parts = jnp.where(place == 2 * number + head, value, parts)
-        rows.append((rough, fine, parts))
-
+        totals.append(jnp.sum(total, axis=1, keepdims=True))
+        sums.append(mixed)
+    peak, total = jnp.concatenate(peaks, axis=0), jnp.concatenate(totals, axis=0)
+    mean = jnp.concatenate(sums, axis=0) / total
+
+    reach = jnp.max(jnp.abs(mean), axis=1, keepdims=True)
+    step = jnp.round(jnp.log2(jnp.maximum(reach, 1e-30)))
+    mean = mean * jnp.exp2(-step)
+    rough = mean.astype(bf16)
+    fine = (mean - rough.astype(f32)).astype(bf16)
+    level = peak * SCALE + jnp.log2(total)
+    high = level.astype(bf16).astype(f32)
+    middle = (level - high).astype(bf16).astype(f32)
+    low = level - high - middle
+    place = iota((TOKENS, HEAD), 1) & 63
+    parts = jnp.zeros((TOKENS, HEAD), f32)
+    for number, value in enumerate((high, middle, low, step)):
+        parts = jnp.where(place == 2 * number, value[:TOKENS], parts)
+        parts = jnp.where(place == 2 * number + 1, value[TOKENS:], parts)
     whole = jnp.concatenate(
-        [
-            jnp.concatenate([rows[h][0], rows[h + 2][0], rows[h][1], rows[h + 2][1], (rows[h][2] + rows[h + 2][2]).astype(bf16)], axis=1)
-            for h in range(2)
-        ],
-        axis=0,
+        [rough[:TOKENS], rough[TOKENS:], fine[:TOKENS], fine[TOKENS:], parts.astype(bf16)], axis=1
     )
 
     first = jnp.dot(near[...], whole, preferred_element_type=f32)
@@ -224,8 +222,7 @@
         in_specs=[whole] * 22,
         out_specs=whole,
         scratch_shapes=[
-            pltpu.VMEM((4, CHUNKS, BLOCK, KEYS), jnp.float32),
-            pltpu.VMEM((16, KEYS, HEAD), jnp.bfloat16),
+            pltpu.VMEM((2, CHUNKS, BLOCK, KEYS), jnp.float32),
             pltpu.VMEM((KEYS, HEAD), jnp.bfloat16),
             pltpu.VMEM((KEYS, HEAD), jnp.bfloat16),
         ],

time: 71.6 us -> 69.8 us (0.975)
  starting transfers between devices: 29.6 us -> 31.4 us
  waiting for transfers between devices: 5.58 us -> 3.83 us
  Pallas kernels: 10.3 us -> 9.07 us
    ppermute x15, waiting for transfers between devices: 3.03 us -> 0.75 us  [swap(): return lax.ppermute(array, 'ctx', [(i, i ^ mask) for i in range(DEVICES)])]
    ppermute x15, starting transfers between devices: 18.1 us -> 19.9 us  [swap(): return lax.ppermute(array, 'ctx', [(i, i ^ mask) for i in range(DEVICES)])]
    pallas_call x1, Pallas kernels: 5.64 us -> 4.38 us  [attend(): pl.pallas_call(attend_kernel, out_shape=jax.ShapeDtypeStruct((TOKENS, 640...]
  transfers between devices with their start and end apart: 16 -> 16, of which waited for: 3 -> 2; matrix products, arithmetic and copies ran while one was open for 0% -> 0% of each run, Pallas kernels for 0% -> 1%
where the time goes in v3:
time: 69.8 us; the launch traced here: 69.6 us
  starting transfers between devices  31.4 us (45%)
  blocking collectives  23.9 us (34%)
  Pallas kernels  9.07 us (13%)
  waiting for transfers between devices  3.83 us (5%)
  between operations  0.79 us (1%)
    all_to_all x1, blocking collectives, per_device(): return combine(lax.all_to_all(partial, 'ctx', 0, 0).astype(jnp.float32))  23.9 us
    ppermute x15, starting transfers between devices, swap(): return lax.ppermute(array, 'ctx', [(i, i ^ mask) for i in range(DEVICES)])  19.9 us
    all_to_all x1, starting transfers between devices, per_device(): everyone = lax.all_to_all(send, 'ctx', 0, 0).reshape(DEVICES * SLOTS, 256)  11.5 us
    pallas_call x1, Pallas kernels, attend(): pl.pallas_call(attend_kernel, out_shape=jax.ShapeDtypeStruct((TOKENS, 640...  4.38 us
    all_to_all x1, waiting for transfers between devices, per_device(): everyone = lax.all_to_all(send, 'ctx', 0, 0).reshape(DEVICES * SLOTS, 256)  3.08 us
    pallas_call x1, Pallas kernels, pack(): pl.pallas_call(pack_kernel, out_shape=[jax.ShapeDtypeStruct((DEVICES, SLO...  2.54 us
    pallas_call x1, Pallas kernels, combine(): pl.pallas_call(combine_kernel, out_shape=jax.ShapeDtypeStruct((SLOTS, 409...  1.8 us
  transfers between devices with their start and end apart: 16, of which 2 were waited for; matrix products, arithmetic and copies ran while one was open for 0% of the time, Pallas kernels for 1%

profile of v3, /device:TPU:1, one launch (start us, length us, event | category | flops | bytes accessed | tf_op | source)
XLA Modules:
  0.0 69.6 jit_solution(17671323122718820351)
XLA Ops:
  0.7 2.5 %pack.1 = (bf16[128,4,256]{2,1,0:T(4,128)(2,1)}, bf16[544,128]{1,0:T(8,128)(2,1)}, bf16[544,128]{1,0:T(8,128)(2,1)}, bf16[544,128]{1,0:T(8,128)(2,1)}, bf16[544,...) custom-call(s32[1]{0:T(128)} %bitcast.head_ref, ...), custom_call_target="tpu_custom_call" | custom-call | bytes 2097152 | tf_op jit(solution)/shard_map/pack/pallas_call | solution.py:65
  3.2 3.1 %collective-permute-start.1 = (bf16[544,128]{1,0:T(8,128)(2,1)}, bf16[544,128]{1,0:T(8,128)(2,1)S(1)}, u32[]{:S(2)}, u32[]{:S(2)}) collective-permute-start(bf16[544,128]{1,0:T(8,128)(2,1)} %get-tuple-element.25), channel_id=1, source_target_pairs={{0,34},{1,35},{2,32},{3,33},{4,38},{5,39},{6,36},{7,37},{8,42},{9,... | collective-permute-start | bytes 417800 | tf_op jit(solution)/shard_map/ppermute | solution.py:30
  6.3 1.5 %collective-permute-start.2 = (bf16[544,128]{1,0:T(8,128)(2,1)}, bf16[544,128]{1,0:T(8,128)(2,1)S(1)}, u32[]{:S(2)}, u32[]{:S(2)}) collective-permute-start(bf16[544,128]{1,0:T(8,128)(2,1)} %get-tuple-element.26), channel_id=1, source_target_pairs={{0,38},{1,39},{2,36},{3,37},{4,34},{5,35},{6,32},{7,33},{8,46},{9,... | collective-permute-start | bytes 417800 | tf_op jit(solution)/shard_map/ppermute | solution.py:30
  7.8 0.8 %collective-permute-start = (bf16[544,128]{1,0:T(8,128)(2,1)}, bf16[544,128]{1,0:T(8,128)(2,1)S(1)}, u32[]{:S(2)}, u32[]{:S(2)}) collective-permute-start(bf16[544,128]{1,0:T(8,128)(2,1)} %get-tuple-element.24), channel_id=1, source_target_pairs={{0,36},{1,37},{2,38},{3,39},{4,32},{5,33},{6,34},{7,35},{8,44},{9,... | collective-permute-start | bytes 417800 | tf_op jit(solution)/shard_map/ppermute | solution.py:30
  8.7 2.6 %collective-permute-start.3 = (bf16[544,128]{1,0:T(8,128)(2,1)}, bf16[544,128]{1,0:T(8,128)(2,1)S(1)}, u32[]{:S(2)}, u32[]{:S(2)}) collective-permute-start(bf16[544,128]{1,0:T(8,128)(2,1)} %get-tuple-element.32), channel_id=1, source_target_pairs={{0,6},{1,7},{2,4},{3,5},{4,2},{5,3},{6,0},{7,1},{8,14},{9,15},{10,... | collective-permute-start | bytes 417800 | tf_op jit(solution)/shard_map/ppermute | solution.py:30
  11.2 1.8 %collective-permute-start.7 = (bf16[544,128]{1,0:T(8,128)(2,1)}, bf16[544,128]{1,0:T(8,128)(2,1)S(1)}, u32[]{:S(2)}, u32[]{:S(2)}) collective-permute-start(bf16[544,128]{1,0:T(8,128)(2,1)} %get-tuple-element.23.rest_0_), channel_id=1, source_target_pairs={{0,1},{1,0},{2,3},{3,2},{4,5},{5,4},{6,7},{7,6},{8,9},{9,8},{10,11... | collective-permute-start | bytes 417800 | tf_op jit(solution)/shard_map/ppermute | solution.py:30
  13.0 11.5 %all-to-all-start = ((bf16[128,4,256]{2,1,0:T(4,128)(2,1)}), bf16[128,4,256]{2,1,0:T(4,128)(2,1)S(1)}, u32[]{:S(2)}, u32[]{:S(2)}) async-start(bf16[128,4,256]{2,1,0:T(4,128)(2,1)} %get-tuple-element.22), calls=%async_computation | async-start | bytes 524288 | tf_op jit(solution)/shard_map/all_to_all | solution.py:281
  24.5 0.0 collective-permute-done.1.rest_2_
  24.6 1.5 %collective-permute-start.4 = (bf16[544,128]{1,0:T(8,128)(2,1)}, bf16[544,128]{1,0:T(8,128)(2,1)S(1)}, u32[]{:S(2)}, u32[]{:S(2)}) collective-permute-start(bf16[544,128]{1,0:T(8,128)(2,1)} %get-tuple-element.34), channel_id=1, source_target_pairs={{0,2},{1,3},{2,0},{3,1},{4,6},{5,7},{6,4},{7,5},{8,10},{9,11},{10,... | collective-permute-start | bytes 417800 | tf_op jit(solution)/shard_map/ppermute | solution.py:30
  26.0 1.4 %collective-permute-start.5 = (bf16[544,128]{1,0:T(8,128)(2,1)S(1)}, bf16[544,128]{1,0:T(8,128)(2,1)S(1)}, u32[]{:S(2)}, u32[]{:S(2)}) collective-permute-start(bf16[544,128]{1,0:T(8,128)(2,1)S(1)} %copy-done.3), channel_id=1, source_target_pairs={{0,32},{1,33},{2,34},{3,35},{4,36},{5,37},{6,38},{7,39},{8,40},{9,... | collective-permute-start | bytes 417800 | tf_op jit(solution)/shard_map/ppermute | solution.py:30
  27.4 0.9 %collective-permute-start.8 = (bf16[544,128]{1,0:T(8,128)(2,1)S(1)}, bf16[544,128]{1,0:T(8,128)(2,1)S(1)}, u32[]{:S(2)}, u32[]{:S(2)}) collective-permute-start(bf16[544,128]{1,0:T(8,128)(2,1)S(1)} %collective-permute-done.rest_1_), channel_id=1, source_target_pairs={{0,1},{1,0},{2,3},{3,2},{4,5},{5,4},{6,7},{7,6},{8,9},{9,8},{10,11... | collective-permute-start | bytes 417800 | tf_op jit(solution)/shard_map/ppermute | solution.py:30
  28.3 0.1 collective-permute-start.9
  28.4 0.0 collective-permute-done.7.rest_8_
  28.4 1.2 %collective-permute-start.6 = (bf16[544,128]{1,0:T(8,128)(2,1)S(1)}, bf16[544,128]{1,0:T(8,128)(2,1)S(1)}, u32[]{:S(2)}, u32[]{:S(2)}) collective-permute-start(bf16[544,128]{1,0:T(8,128)(2,1)S(1)} %copy-done.2), channel_id=1, source_target_pairs={{0,4},{1,5},{2,6},{3,7},{4,0},{5,1},{6,2},{7,3},{8,12},{9,13},{10,... | collective-permute-start | bytes 417800 | tf_op jit(solution)/shard_map/ppermute | solution.py:30
  29.7 0.1 copy.8.col_ref
  29.8 0.0 collective-permute-done.8.rest_9_
  29.8 0.8 %collective-permute-start.10 = (bf16[544,128]{1,0:T(8,128)(2,1)S(1)}, bf16[544,128]{1,0:T(8,128)(2,1)S(1)}, u32[]{:S(2)}, u32[]{:S(2)}) collective-permute-start(bf16[544,128]{1,0:T(8,128)(2,1)S(1)} %collective-permute-done.2.rest_3_), channel_id=1, source_target_pairs={{0,1},{1,0},{2,3},{3,2},{4,5},{5,4},{6,7},{7,6},{8,9},{9,8},{10,11... | collective-permute-start | bytes 417800 | tf_op jit(solution)/shard_map/ppermute | solution.py:30
  30.6 0.0 collective-permute-done.4.rest_5_
  30.6 2.1 %collective-permute-start.11 = (bf16[544,128]{1,0:T(8,128)(2,1)S(1)}, bf16[544,128]{1,0:T(8,128)(2,1)S(1)}, u32[]{:S(2)}, u32[]{:S(2)}) collective-permute-start(bf16[544,128]{1,0:T(8,128)(2,1)S(1)} %collective-permute-done.3.rest_4_), channel_id=1, source_target_pairs={{0,1},{1,0},{2,3},{3,2},{4,5},{5,4},{6,7},{7,6},{8,9},{9,8},{10,11... | collective-permute-start | bytes 417800 | tf_op jit(solution)/shard_map/ppermute | solution.py:30
  32.7 0.0 collective-permute-done.9.rest_10_
  32.7 0.0 collective-permute-start.12
  32.7 1.2 %collective-permute-start.13 = (bf16[544,128]{1,0:T(8,128)(2,1)S(1)}, bf16[544,128]{1,0:T(8,128)(2,1)S(1)}, u32[]{:S(2)}, u32[]{:S(2)}) collective-permute-start(bf16[544,128]{1,0:T(8,128)(2,1)S(1)} %collective-permute-done.5.rest_6_), channel_id=1, source_target_pairs={{0,1},{1,0},{2,3},{3,2},{4,5},{5,4},{6,7},{7,6},{8,9},{9,8},{10,11... | collective-permute-start | bytes 417800 | tf_op jit(solution)/shard_map/ppermute | solution.py:30
  33.9 0.7 %collective-permute-done.6.rest_7_ = bf16[544,128]{1,0:T(8,128)(2,1)S(1)} collective-permute-done((bf16[544,128]{1,0:T(8,128)(2,1)S(1)}, bf16[544,128]{1,0:T(8,128)(2,1)S(1)}, u32[]{:S(2)}, u32[]{:S(2)}) %collective-permute-start.6) | collective-permute-done | bytes 139296 | tf_op jit(solution)/shard_map/ppermute | solution.py:30
  34.6 0.9 %collective-permute-start.14 = (bf16[544,128]{1,0:T(8,128)(2,1)S(1)}, bf16[544,128]{1,0:T(8,128)(2,1)S(1)}, u32[]{:S(2)}, u32[]{:S(2)}) collective-permute-start(bf16[544,128]{1,0:T(8,128)(2,1)S(1)} %collective-permute-done.6.rest_7_), channel_id=1, source_target_pairs={{0,1},{1,0},{2,3},{3,2},{4,5},{5,4},{6,7},{7,6},{8,9},{9,8},{10,11... | collective-permute-start | bytes 417800 | tf_op jit(solution)/shard_map/ppermute | solution.py:30
  35.5 0.4 prepare.1
  35.9 3.1 %all-to-all-done = bf16[128,4,256]{2,1,0:T(4,128)(2,1)S(1)} async-done(((bf16[128,4,256]{2,1,0:T(4,128)(2,1)}), bf16[128,4,256]{2,1,0:T(4,128)(2,1)S(1)}, u32[]{:S(2)}, u32[]{:S(2)}) %all-to-all-start) | async-done | bytes 262176 | tf_op jit(solution)/shard_map/all_to_all | solution.py:281
  38.9 0.1 reshape.9.q_ref
  39.1 4.4 %attend.1 = f32[256,640]{1,0:T(8,128)S(1)} custom-call(bf16[512,256]{1,0:T(8,128)(2,1)S(1)} %reshape.9.q_ref, bf16[256,512]{1,0:T(8,128)(2,1)S(1)} %get-tuple-element.27.pick, bf16[256,256]{1,0:T(8,128)(2,1)S(1)} %get-tuple-element.28.near, bf16[256,256]{1,0:T(8,128)(2,1)S(1)} %get-tuple-element.29.far, f32[1,256]{1,0:T(1,128)S(1)} %get-tuple-element.30.token_ref, ...), custom_call_target="tpu_custom_call" | custom-call | flops 1140850688 | bytes 3145728 | tf_op jit(solution)/shard_map/attend/pallas_call | solution.py:219
  43.5 0.2 reshape.11
  43.7 23.9 %all_to_all.10 = f16[128,2,640]{2,1,0:T(2,128)(2,1)S(1)} all-to-all(f16[128,2,640]{2,1,0:T(2,128)(2,1)S(1)} %reshape.11), channel_id=1, replica_groups=mesh['batch'=2,'ctx'=128] {'ctx'}, dimensions={0} | all-to-all | bytes 655360 | tf_op jit(solution)/shard_map/all_to_all | solution.py:285
  67.5 0.2 convert_element_type.7.parts_ref
  67.8 1.8 %combine.1 = bf16[4,4096]{1,0:T(4,128)(2,1)} custom-call(f32[128,2,640]{2,1,0:T(2,128)S(1)} %convert_element_type.7.parts_ref), custom_call_target="tpu_custom_call" | custom-call | tf_op jit(solution)/shard_map/combine/pallas_call | solution.py:257
  (18 shorter events, 0.1 us)
Async XLA Ops:
  3.2 21.3 %collective-permute-start.1 = (bf16[544,128]{1,0:T(8,128)(2,1)}, bf16[544,128]{1,0:T(8,128)(2,1)S(1)}, u32[]{:S(2)}, u32[]{:S(2)}) collective-permute-start(bf16[544,128]{1,0:T(8,128)(2,1)} %get-tuple-element.25), channel_id=1, source_target_pairs={{0,34},{1,35},{2,32},{3,33},{4,38},{5,39},{6,36},{7,37},{8,42},{9,... | collective-permute-start | bytes 417800 | tf_op jit(solution)/shard_map/ppermute | solution.py:30
  6.3 19.7 %collective-permute-start.2 = (bf16[544,128]{1,0:T(8,128)(2,1)}, bf16[544,128]{1,0:T(8,128)(2,1)S(1)}, u32[]{:S(2)}, u32[]{:S(2)}) collective-permute-start(bf16[544,128]{1,0:T(8,128)(2,1)} %get-tuple-element.26), channel_id=1, source_target_pairs={{0,38},{1,39},{2,36},{3,37},{4,34},{5,35},{6,32},{7,33},{8,46},{9,... | collective-permute-start | bytes 417800 | tf_op jit(solution)/shard_map/ppermute | solution.py:30
  7.8 19.6 %collective-permute-start = (bf16[544,128]{1,0:T(8,128)(2,1)}, bf16[544,128]{1,0:T(8,128)(2,1)S(1)}, u32[]{:S(2)}, u32[]{:S(2)}) collective-permute-start(bf16[544,128]{1,0:T(8,128)(2,1)} %get-tuple-element.24), channel_id=1, source_target_pairs={{0,36},{1,37},{2,38},{3,39},{4,32},{5,33},{6,34},{7,35},{8,44},{9,... | collective-permute-start | bytes 417800 | tf_op jit(solution)/shard_map/ppermute | solution.py:30
  8.7 19.7 %collective-permute-start.3 = (bf16[544,128]{1,0:T(8,128)(2,1)}, bf16[544,128]{1,0:T(8,128)(2,1)S(1)}, u32[]{:S(2)}, u32[]{:S(2)}) collective-permute-start(bf16[544,128]{1,0:T(8,128)(2,1)} %get-tuple-element.32), channel_id=1, source_target_pairs={{0,6},{1,7},{2,4},{3,5},{4,2},{5,3},{6,0},{7,1},{8,14},{9,15},{10,... | collective-permute-start | bytes 417800 | tf_op jit(solution)/shard_map/ppermute | solution.py:30
  11.2 17.2 %collective-permute-start.7 = (bf16[544,128]{1,0:T(8,128)(2,1)}, bf16[544,128]{1,0:T(8,128)(2,1)S(1)}, u32[]{:S(2)}, u32[]{:S(2)}) collective-permute-start(bf16[544,128]{1,0:T(8,128)(2,1)} %get-tuple-element.23.rest_0_), channel_id=1, source_target_pairs={{0,1},{1,0},{2,3},{3,2},{4,5},{5,4},{6,7},{7,6},{8,9},{9,8},{10,11... | collective-permute-start | bytes 417800 | tf_op jit(solution)/shard_map/ppermute | solution.py:30
  13.0 13.0 %copy-start.3 = (bf16[544,128]{1,0:T(8,128)(2,1)S(1)}, bf16[544,128]{1,0:T(8,128)(2,1)}, u32[]{:S(2)}) copy-start(bf16[544,128]{1,0:T(8,128)(2,1)} %get-tuple-element.36) | copy-start | bytes 417796
  13.0 15.4 %copy-start.2 = (bf16[544,128]{1,0:T(8,128)(2,1)S(1)}, bf16[544,128]{1,0:T(8,128)(2,1)}, u32[]{:S(2)}) copy-start(bf16[544,128]{1,0:T(8,128)(2,1)} %get-tuple-element.38) | copy-start | bytes 417796
  13.0 22.5 %copy-start.1 = (bf16[544,128]{1,0:T(8,128)(2,1)S(1)}, bf16[544,128]{1,0:T(8,128)(2,1)}, u32[]{:S(2)}) copy-start(bf16[544,128]{1,0:T(8,128)(2,1)} %get-tuple-element.23.rest_0_) | copy-start | bytes 417796
  13.0 25.9 %all-to-all-start = ((bf16[128,4,256]{2,1,0:T(4,128)(2,1)}), bf16[128,4,256]{2,1,0:T(4,128)(2,1)S(1)}, u32[]{:S(2)}, u32[]{:S(2)}) async-start(bf16[128,4,256]{2,1,0:T(4,128)(2,1)} %get-tuple-element.22), calls=%async_computation | async-start | bytes 524288 | tf_op jit(solution)/shard_map/all_to_all | solution.py:281
  24.6 6.0 %collective-permute-start.4 = (bf16[544,128]{1,0:T(8,128)(2,1)}, bf16[544,128]{1,0:T(8,128)(2,1)S(1)}, u32[]{:S(2)}, u32[]{:S(2)}) collective-permute-start(bf16[544,128]{1,0:T(8,128)(2,1)} %get-tuple-element.34), channel_id=1, source_target_pairs={{0,2},{1,3},{2,0},{3,1},{4,6},{5,7},{6,4},{7,5},{8,10},{9,11},{10,... | collective-permute-start | bytes 417800 | tf_op jit(solution)/shard_map/ppermute | solution.py:30
  26.0 3.6 %copy-start = (s32[256,1]{0,1:T(1,128)S(1)}, s32[256,1]{0,1:T(1,128)}, u32[]{:S(2)}) copy-start(s32[256,1]{0,1:T(1,128)} %param.8) | copy-start | bytes 3076
  26.0 6.7 %collective-permute-start.5 = (bf16[544,128]{1,0:T(8,128)(2,1)S(1)}, bf16[544,128]{1,0:T(8,128)(2,1)S(1)}, u32[]{:S(2)}, u32[]{:S(2)}) collective-permute-start(bf16[544,128]{1,0:T(8,128)(2,1)S(1)} %copy-done.3), channel_id=1, source_target_pairs={{0,32},{1,33},{2,34},{3,35},{4,36},{5,37},{6,38},{7,39},{8,40},{9,... | collective-permute-start | bytes 417800 | tf_op jit(solution)/shard_map/ppermute | solution.py:30
  27.4 2.4 %collective-permute-start.8 = (bf16[544,128]{1,0:T(8,128)(2,1)S(1)}, bf16[544,128]{1,0:T(8,128)(2,1)S(1)}, u32[]{:S(2)}, u32[]{:S(2)}) collective-permute-start(bf16[544,128]{1,0:T(8,128)(2,1)S(1)} %collective-permute-done.rest_1_), channel_id=1, source_target_pairs={{0,1},{1,0},{2,3},{3,2},{4,5},{5,4},{6,7},{7,6},{8,9},{9,8},{10,11... | collective-permute-start | bytes 417800 | tf_op jit(solution)/shard_map/ppermute | solution.py:30
  28.3 4.3 %collective-permute-start.9 = (bf16[544,128]{1,0:T(8,128)(2,1)S(1)}, bf16[544,128]{1,0:T(8,128)(2,1)S(1)}, u32[]{:S(2)}, u32[]{:S(2)}) collective-permute-start(bf16[544,128]{1,0:T(8,128)(2,1)S(1)} %collective-permute-done.1.rest_2_), channel_id=1, source_target_pairs={{0,1},{1,0},{2,3},{3,2},{4,5},{5,4},{6,7},{7,6},{8,9},{9,8},{10,11... | collective-permute-start | bytes 417800 | tf_op jit(solution)/shard_map/ppermute | solution.py:30
  28.4 6.2 %collective-permute-start.6 = (bf16[544,128]{1,0:T(8,128)(2,1)S(1)}, bf16[544,128]{1,0:T(8,128)(2,1)S(1)}, u32[]{:S(2)}, u32[]{:S(2)}) collective-permute-start(bf16[544,128]{1,0:T(8,128)(2,1)S(1)} %copy-done.2), channel_id=1, source_target_pairs={{0,4},{1,5},{2,6},{3,7},{4,0},{5,1},{6,2},{7,3},{8,12},{9,13},{10,... | collective-permute-start | bytes 417800 | tf_op jit(solution)/shard_map/ppermute | solution.py:30
  29.8 9.2 %collective-permute-start.10 = (bf16[544,128]{1,0:T(8,128)(2,1)S(1)}, bf16[544,128]{1,0:T(8,128)(2,1)S(1)}, u32[]{:S(2)}, u32[]{:S(2)}) collective-permute-start(bf16[544,128]{1,0:T(8,128)(2,1)S(1)} %collective-permute-done.2.rest_3_), channel_id=1, source_target_pairs={{0,1},{1,0},{2,3},{3,2},{4,5},{5,4},{6,7},{7,6},{8,9},{9,8},{10,11... | collective-permute-start | bytes 417800 | tf_op jit(solution)/shard_map/ppermute | solution.py:30
  30.6 8.4 %collective-permute-start.11 = (bf16[544,128]{1,0:T(8,128)(2,1)S(1)}, bf16[544,128]{1,0:T(8,128)(2,1)S(1)}, u32[]{:S(2)}, u32[]{:S(2)}) collective-permute-start(bf16[544,128]{1,0:T(8,128)(2,1)S(1)} %collective-permute-done.3.rest_4_), channel_id=1, source_target_pairs={{0,1},{1,0},{2,3},{3,2},{4,5},{5,4},{6,7},{7,6},{8,9},{9,8},{10,11... | collective-permute-start | bytes 417800 | tf_op jit(solution)/shard_map/ppermute | solution.py:30
  32.7 6.4 %collective-permute-start.12 = (bf16[544,128]{1,0:T(8,128)(2,1)S(1)}, bf16[544,128]{1,0:T(8,128)(2,1)S(1)}, u32[]{:S(2)}, u32[]{:S(2)}) collective-permute-start(bf16[544,128]{1,0:T(8,128)(2,1)S(1)} %collective-permute-done.4.rest_5_), channel_id=1, source_target_pairs={{0,1},{1,0},{2,3},{3,2},{4,5},{5,4},{6,7},{7,6},{8,9},{9,8},{10,11... | collective-permute-start | bytes 417800 | tf_op jit(solution)/shard_map/ppermute | solution.py:30
  32.7 6.4 %collective-permute-start.13 = (bf16[544,128]{1,0:T(8,128)(2,1)S(1)}, bf16[544,128]{1,0:T(8,128)(2,1)S(1)}, u32[]{:S(2)}, u32[]{:S(2)}) collective-permute-start(bf16[544,128]{1,0:T(8,128)(2,1)S(1)} %collective-permute-done.5.rest_6_), channel_id=1, source_target_pairs={{0,1},{1,0},{2,3},{3,2},{4,5},{5,4},{6,7},{7,6},{8,9},{9,8},{10,11... | collective-permute-start | bytes 417800 | tf_op jit(solution)/shard_map/ppermute | solution.py:30
  34.6 4.4 %collective-permute-start.14 = (bf16[544,128]{1,0:T(8,128)(2,1)S(1)}, bf16[544,128]{1,0:T(8,128)(2,1)S(1)}, u32[]{:S(2)}, u32[]{:S(2)}) collective-permute-start(bf16[544,128]{1,0:T(8,128)(2,1)S(1)} %collective-permute-done.6.rest_7_), channel_id=1, source_target_pairs={{0,1},{1,0},{2,3},{3,2},{4,5},{5,4},{6,7},{7,6},{8,9},{9,8},{10,11... | collective-permute-start | bytes 417800 | tf_op jit(solution)/shard_map/ppermute | solution.py:30

commit v4 on v3

--- a/solution.py
+++ b/solution.py
@@ -13,12 +13,12 @@
 TOKENS = 256
 KEYS = 256
 DEVICES = 128
-CHIP_MASKS = tuple((d >> 2) * 32 + (d >> 1 & 1) * 4 + (d & 1) * 2 for d in range(8))
-ORDER = (0, 6, 5, 7, 3, 1, 4, 2)
+CHIP_MASKS = tuple((d >> 1) * 32 + (d & 1) * 2 for d in range(8))
+ORDER = (0, 7, 3, 5, 4, 1, 6, 2)
 EARLY = 4
 AFTER = (0, 0, 0, 0, 0, 2, 3, 4)
 PREPARE_FLOPS = 2850000000
-PACK_LIMIT = 60
+PACK_LIMIT = 56
 PIECE = 2 * KEYS + 32
 CHUNKS = 17
 BLOCK = 256
@@ -39,7 +39,7 @@
     queries, new_keys, new_values, keys, values = held
     fetches[0].wait()
     for device in range(DEVICES):
-        at = ((device >> 5 & 1) * 8 + (device >> 2 & 1) * 4 + (device & 3)) * 256
+        at = ((device >> 5) * 4 + (device & 3)) * 256
         send[device] = queries[:, at : at + 256]
     width = KV_HEADS * HEAD
     fetches[1].wait()
@@ -235,17 +235,17 @@
 
 
 def combine_kernel(parts_ref, out_ref, whole):
-    split = lambda array: array.reshape(2, 2, 4, 8, 2, array.shape[-1])
+    split = lambda array: array.reshape(4, 8, 4, 2, array.shape[-1])
     levels = parts_ref[:, :, 512:640]
     ahead = lambda count: pltpu.roll(levels, HEAD - count, 2)
     step = jnp.exp2(ahead(6))
     level = split(levels + ahead(2) + ahead(4))
-    factor = jnp.exp2(level - jnp.max(level, axis=(0, 2), keepdims=True))
-    factor = factor / jnp.sum(factor, axis=(0, 2), keepdims=True) * split(step)
+    factor = jnp.exp2(level - jnp.max(level, axis=1, keepdims=True))
+    factor = factor / jnp.sum(factor, axis=1, keepdims=True) * split(step)
     for v in range(4):
         at = 64 * (v // 2) + v % 2
         mean = split(parts_ref[:, :, v * HEAD : (v + 1) * HEAD])
-        mean = jnp.sum(mean * factor[..., at : at + 1], axis=(0, 2)).reshape(16, 2, HEAD)
+        mean = jnp.sum(mean * factor[..., at : at + 1], axis=1).reshape(16, 2, HEAD)
         for pair in range(16):
             column = pair * 256 + v % 2 * HEAD
             whole[v // 2 * 2 : v // 2 * 2 + 2, column : column + HEAD] = mean[pair]
@@ -268,7 +268,7 @@
 def per_device(queries, owners, new_keys, new_values, cache_keys, cache_values, lengths):
     bf16 = jnp.bfloat16
     here = lax.axis_index("ctx").astype(jnp.int32)
-    head = (here >> 5 & 1) * 4 + (here >> 2 & 1) * 2 + (here >> 1 & 1)
+    head = (here >> 5) * 2 + (here >> 1 & 1)
 
     send, *mine = pack(head[None], lengths, queries, new_keys, new_values, cache_keys, cache_values)
     held = [mine[0]]

time: 69.8 us -> 68.8 us (0.986)
  blocking collectives: 23.9 us -> 22.9 us
    ppermute x15, waiting for transfers between devices: 0.75 us -> 2.44 us  [swap(): return lax.ppermute(array, 'ctx', [(i, i ^ mask) for i in range(DEVICES)])]
    all_to_all x1, waiting for transfers between devices: 3.08 us -> 1.6 us  [per_device(): everyone = lax.all_to_all(send, 'ctx', 0, 0).reshape(DEVICES * SLOTS, 256)]
    all_to_all x1, blocking collectives: 23.9 us -> 22.9 us  [per_device(): return combine(lax.all_to_all(partial, 'ctx', 0, 0).astype(jnp.float32))]
  transfers between devices with their start and end apart: 16 -> 16, of which waited for: 2 -> 4; matrix products, arithmetic and copies ran while one was open for 0% -> 0% of each run, Pallas kernels for 1% -> 1%
where the time goes in v4:
time: 68.8 us; the launch traced here: 68.6 us
  starting transfers between devices  31.2 us (45%)
  blocking collectives  22.9 us (33%)
  Pallas kernels  8.99 us (13%)
  waiting for transfers between devices  4.04 us (6%)
  between operations  0.79 us (1%)
    all_to_all x1, blocking collectives, per_device(): return combine(lax.all_to_all(partial, 'ctx', 0, 0).astype(jnp.float32))  22.9 us
    ppermute x15, starting transfers between devices, swap(): return lax.ppermute(array, 'ctx', [(i, i ^ mask) for i in range(DEVICES)])  19.8 us
    all_to_all x1, starting transfers between devices, per_device(): everyone = lax.all_to_all(send, 'ctx', 0, 0).reshape(DEVICES * SLOTS, 256)  11.4 us
    pallas_call x1, Pallas kernels, attend(): pl.pallas_call(attend_kernel, out_shape=jax.ShapeDtypeStruct((TOKENS, 640...  4.38 us
    pallas_call x1, Pallas kernels, pack(): pl.pallas_call(pack_kernel, out_shape=[jax.ShapeDtypeStruct((DEVICES, SLO...  2.54 us
    ppermute x15, waiting for transfers between devices, swap(): return lax.ppermute(array, 'ctx', [(i, i ^ mask) for i in range(DEVICES)])  2.44 us
    pallas_call x1, Pallas kernels, combine(): pl.pallas_call(combine_kernel, out_shape=jax.ShapeDtypeStruct((SLOTS, 409...  1.72 us
    all_to_all x1, waiting for transfers between devices, per_device(): everyone = lax.all_to_all(send, 'ctx', 0, 0).reshape(DEVICES * SLOTS, 256)  1.6 us
  transfers between devices with their start and end apart: 16, of which 4 were waited for; matrix products, arithmetic and copies ran while one was open for 0% of the time, Pallas kernels for 1%

profile of v4, /device:TPU:1, one launch (start us, length us, event | category | flops | bytes accessed | tf_op | source)
XLA Modules:
  0.0 68.6 jit_solution(15778760869750460857)
XLA Ops:
  0.7 2.5 %pack.1 = (bf16[128,4,256]{2,1,0:T(4,128)(2,1)}, bf16[544,128]{1,0:T(8,128)(2,1)}, bf16[544,128]{1,0:T(8,128)(2,1)}, bf16[544,128]{1,0:T(8,128)(2,1)}, bf16[544,...) custom-call(s32[1]{0:T(128)} %bitcast.head_ref, ...), custom_call_target="tpu_custom_call" | custom-call | bytes 2097152 | tf_op jit(solution)/shard_map/pack/pallas_call | solution.py:65
  3.2 3.1 %collective-permute-start.1 = (bf16[544,128]{1,0:T(8,128)(2,1)}, bf16[544,128]{1,0:T(8,128)(2,1)S(1)}, u32[]{:S(2)}, u32[]{:S(2)}) collective-permute-start(bf16[544,128]{1,0:T(8,128)(2,1)} %get-tuple-element.25), channel_id=1, source_target_pairs={{0,34},{1,35},{2,32},{3,33},{4,38},{5,39},{6,36},{7,37},{8,42},{9,... | collective-permute-start | bytes 417800 | tf_op jit(solution)/shard_map/ppermute | solution.py:30
  6.3 2.6 %collective-permute-start.2 = (bf16[544,128]{1,0:T(8,128)(2,1)}, bf16[544,128]{1,0:T(8,128)(2,1)S(1)}, u32[]{:S(2)}, u32[]{:S(2)}) collective-permute-start(bf16[544,128]{1,0:T(8,128)(2,1)} %get-tuple-element.26), channel_id=1, source_target_pairs={{0,66},{1,67},{2,64},{3,65},{4,70},{5,71},{6,68},{7,69},{8,74},{9,... | collective-permute-start | bytes 417800 | tf_op jit(solution)/shard_map/ppermute | solution.py:30
  8.9 0.9 %collective-permute-start = (bf16[544,128]{1,0:T(8,128)(2,1)}, bf16[544,128]{1,0:T(8,128)(2,1)S(1)}, u32[]{:S(2)}, u32[]{:S(2)}) collective-permute-start(bf16[544,128]{1,0:T(8,128)(2,1)} %get-tuple-element.24), channel_id=1, source_target_pairs={{0,98},{1,99},{2,96},{3,97},{4,102},{5,103},{6,100},{7,101},{8,106... | collective-permute-start | bytes 417800 | tf_op jit(solution)/shard_map/ppermute | solution.py:30
  9.8 1.7 %collective-permute-start.3 = (bf16[544,128]{1,0:T(8,128)(2,1)}, bf16[544,128]{1,0:T(8,128)(2,1)S(1)}, u32[]{:S(2)}, u32[]{:S(2)}) collective-permute-start(bf16[544,128]{1,0:T(8,128)(2,1)} %get-tuple-element.32), channel_id=1, source_target_pairs={{0,64},{1,65},{2,66},{3,67},{4,68},{5,69},{6,70},{7,71},{8,72},{9,... | collective-permute-start | bytes 417800 | tf_op jit(solution)/shard_map/ppermute | solution.py:30
  11.5 1.8 %collective-permute-start.7 = (bf16[544,128]{1,0:T(8,128)(2,1)}, bf16[544,128]{1,0:T(8,128)(2,1)S(1)}, u32[]{:S(2)}, u32[]{:S(2)}) collective-permute-start(bf16[544,128]{1,0:T(8,128)(2,1)} %get-tuple-element.23.rest_0_), channel_id=1, source_target_pairs={{0,1},{1,0},{2,3},{3,2},{4,5},{5,4},{6,7},{7,6},{8,9},{9,8},{10,11... | collective-permute-start | bytes 417800 | tf_op jit(solution)/shard_map/ppermute | solution.py:30
  13.3 11.4 %all-to-all-start = ((bf16[128,4,256]{2,1,0:T(4,128)(2,1)}), bf16[128,4,256]{2,1,0:T(4,128)(2,1)S(1)}, u32[]{:S(2)}, u32[]{:S(2)}) async-start(bf16[128,4,256]{2,1,0:T(4,128)(2,1)} %get-tuple-element.22), calls=%async_computation | async-start | bytes 524288 | tf_op jit(solution)/shard_map/all_to_all | solution.py:281
  24.7 1.5 %collective-permute-start.4 = (bf16[544,128]{1,0:T(8,128)(2,1)}, bf16[544,128]{1,0:T(8,128)(2,1)S(1)}, u32[]{:S(2)}, u32[]{:S(2)}) collective-permute-start(bf16[544,128]{1,0:T(8,128)(2,1)} %get-tuple-element.34), channel_id=1, source_target_pairs={{0,2},{1,3},{2,0},{3,1},{4,6},{5,7},{6,4},{7,5},{8,10},{9,11},{10,... | collective-permute-start | bytes 417800 | tf_op jit(solution)/shard_map/ppermute | solution.py:30
  26.2 0.0 collective-permute-done.2.rest_3_
  26.2 3.0 %collective-permute-start.5 = (bf16[544,128]{1,0:T(8,128)(2,1)S(1)}, bf16[544,128]{1,0:T(8,128)(2,1)S(1)}, u32[]{:S(2)}, u32[]{:S(2)}) collective-permute-start(bf16[544,128]{1,0:T(8,128)(2,1)S(1)} %copy-done.3), channel_id=1, source_target_pairs={{0,96},{1,97},{2,98},{3,99},{4,100},{5,101},{6,102},{7,103},{8,104... | collective-permute-start | bytes 417800 | tf_op jit(solution)/shard_map/ppermute | solution.py:30
  29.2 0.0 collective-permute-done.rest_1_
  29.2 0.9 %collective-permute-start.8 = (bf16[544,128]{1,0:T(8,128)(2,1)S(1)}, bf16[544,128]{1,0:T(8,128)(2,1)S(1)}, u32[]{:S(2)}, u32[]{:S(2)}) collective-permute-start(bf16[544,128]{1,0:T(8,128)(2,1)S(1)} %collective-permute-done.rest_1_), channel_id=1, source_target_pairs={{0,1},{1,0},{2,3},{3,2},{4,5},{5,4},{6,7},{7,6},{8,9},{9,8},{10,11... | collective-permute-start | bytes 417800 | tf_op jit(solution)/shard_map/ppermute | solution.py:30
  30.1 0.0 collective-permute-done.3.rest_4_
  30.1 0.1 collective-permute-start.9
  30.2 0.0 collective-permute-start.6
  30.3 0.1 copy.8.col_ref
  30.4 0.7 %collective-permute-done.8.rest_9_ = bf16[544,128]{1,0:T(8,128)(2,1)S(1)} collective-permute-done((bf16[544,128]{1,0:T(8,128)(2,1)S(1)}, bf16[544,128]{1,0:T(8,128)(2,1)S(1)}, u32[]{:S(2)}, u32[]{:S(2)}) %collective-permute-start.8) | collective-permute-done | bytes 139296 | tf_op jit(solution)/shard_map/ppermute | solution.py:30
  31.1 0.4 collective-permute-start.10
  31.5 1.3 %collective-permute-start.11 = (bf16[544,128]{1,0:T(8,128)(2,1)S(1)}, bf16[544,128]{1,0:T(8,128)(2,1)S(1)}, u32[]{:S(2)}, u32[]{:S(2)}) collective-permute-start(bf16[544,128]{1,0:T(8,128)(2,1)S(1)} %collective-permute-done.3.rest_4_), channel_id=1, source_target_pairs={{0,1},{1,0},{2,3},{3,2},{4,5},{5,4},{6,7},{7,6},{8,9},{9,8},{10,11... | collective-permute-start | bytes 417800 | tf_op jit(solution)/shard_map/ppermute | solution.py:30
  32.8 0.0 collective-permute-start.12
  32.8 1.5 %collective-permute-done.5.rest_6_ = bf16[544,128]{1,0:T(8,128)(2,1)S(1)} collective-permute-done((bf16[544,128]{1,0:T(8,128)(2,1)S(1)}, bf16[544,128]{1,0:T(8,128)(2,1)S(1)}, u32[]{:S(2)}, u32[]{:S(2)}) %collective-permute-start.5) | collective-permute-done | bytes 139296 | tf_op jit(solution)/shard_map/ppermute | solution.py:30
  34.3 1.3 %collective-permute-start.13 = (bf16[544,128]{1,0:T(8,128)(2,1)S(1)}, bf16[544,128]{1,0:T(8,128)(2,1)S(1)}, u32[]{:S(2)}, u32[]{:S(2)}) collective-permute-start(bf16[544,128]{1,0:T(8,128)(2,1)S(1)} %collective-permute-done.5.rest_6_), channel_id=1, source_target_pairs={{0,1},{1,0},{2,3},{3,2},{4,5},{5,4},{6,7},{7,6},{8,9},{9,8},{10,11... | collective-permute-start | bytes 417800 | tf_op jit(solution)/shard_map/ppermute | solution.py:30
  35.7 0.2 collective-permute-done.6.rest_7_
  35.9 1.1 %collective-permute-start.14 = (bf16[544,128]{1,0:T(8,128)(2,1)S(1)}, bf16[544,128]{1,0:T(8,128)(2,1)S(1)}, u32[]{:S(2)}, u32[]{:S(2)}) collective-permute-start(bf16[544,128]{1,0:T(8,128)(2,1)S(1)} %collective-permute-done.6.rest_7_), channel_id=1, source_target_pairs={{0,1},{1,0},{2,3},{3,2},{4,5},{5,4},{6,7},{7,6},{8,9},{9,8},{10,11... | collective-permute-start | bytes 417800 | tf_op jit(solution)/shard_map/ppermute | solution.py:30
  37.0 0.4 prepare.1
  37.4 1.6 %all-to-all-done = bf16[128,4,256]{2,1,0:T(4,128)(2,1)S(1)} async-done(((bf16[128,4,256]{2,1,0:T(4,128)(2,1)}), bf16[128,4,256]{2,1,0:T(4,128)(2,1)S(1)}, u32[]{:S(2)}, u32[]{:S(2)}) %all-to-all-start) | async-done | bytes 262176 | tf_op jit(solution)/shard_map/all_to_all | solution.py:281
  39.0 0.1 reshape.9.q_ref
  39.1 4.4 %attend.1 = f32[256,640]{1,0:T(8,128)S(1)} custom-call(bf16[512,256]{1,0:T(8,128)(2,1)S(1)} %reshape.9.q_ref, bf16[256,512]{1,0:T(8,128)(2,1)S(1)} %get-tuple-element.27.pick, bf16[256,256]{1,0:T(8,128)(2,1)S(1)} %get-tuple-element.28.near, bf16[256,256]{1,0:T(8,128)(2,1)S(1)} %get-tuple-element.29.far, f32[1,256]{1,0:T(1,128)S(1)} %get-tuple-element.30.token_ref, ...), custom_call_target="tpu_custom_call" | custom-call | flops 1140850688 | bytes 3145728 | tf_op jit(solution)/shard_map/attend/pallas_call | solution.py:219
  43.5 0.2 reshape.11
  43.7 22.9 %all_to_all.10 = f16[128,2,640]{2,1,0:T(2,128)(2,1)S(1)} all-to-all(f16[128,2,640]{2,1,0:T(2,128)(2,1)S(1)} %reshape.11), channel_id=1, replica_groups=mesh['batch'=2,'ctx'=128] {'ctx'}, dimensions={0} | all-to-all | bytes 655360 | tf_op jit(solution)/shard_map/all_to_all | solution.py:285
  66.6 0.2 convert_element_type.7.parts_ref
  66.9 1.7 %combine.1 = bf16[4,4096]{1,0:T(4,128)(2,1)} custom-call(f32[128,2,640]{2,1,0:T(2,128)S(1)} %convert_element_type.7.parts_ref), custom_call_target="tpu_custom_call" | custom-call | tf_op jit(solution)/shard_map/combine/pallas_call | solution.py:257
  (18 shorter events, 0.1 us)
Async XLA Ops:
  3.2 21.5 %collective-permute-start.1 = (bf16[544,128]{1,0:T(8,128)(2,1)}, bf16[544,128]{1,0:T(8,128)(2,1)S(1)}, u32[]{:S(2)}, u32[]{:S(2)}) collective-permute-start(bf16[544,128]{1,0:T(8,128)(2,1)} %get-tuple-element.25), channel_id=1, source_target_pairs={{0,34},{1,35},{2,32},{3,33},{4,38},{5,39},{6,36},{7,37},{8,42},{9,... | collective-permute-start | bytes 417800 | tf_op jit(solution)/shard_map/ppermute | solution.py:30
  6.3 19.8 %collective-permute-start.2 = (bf16[544,128]{1,0:T(8,128)(2,1)}, bf16[544,128]{1,0:T(8,128)(2,1)S(1)}, u32[]{:S(2)}, u32[]{:S(2)}) collective-permute-start(bf16[544,128]{1,0:T(8,128)(2,1)} %get-tuple-element.26), channel_id=1, source_target_pairs={{0,66},{1,67},{2,64},{3,65},{4,70},{5,71},{6,68},{7,69},{8,74},{9,... | collective-permute-start | bytes 417800 | tf_op jit(solution)/shard_map/ppermute | solution.py:30
  8.9 20.3 %collective-permute-start = (bf16[544,128]{1,0:T(8,128)(2,1)}, bf16[544,128]{1,0:T(8,128)(2,1)S(1)}, u32[]{:S(2)}, u32[]{:S(2)}) collective-permute-start(bf16[544,128]{1,0:T(8,128)(2,1)} %get-tuple-element.24), channel_id=1, source_target_pairs={{0,98},{1,99},{2,96},{3,97},{4,102},{5,103},{6,100},{7,101},{8,106... | collective-permute-start | bytes 417800 | tf_op jit(solution)/shard_map/ppermute | solution.py:30
  9.8 20.3 %collective-permute-start.3 = (bf16[544,128]{1,0:T(8,128)(2,1)}, bf16[544,128]{1,0:T(8,128)(2,1)S(1)}, u32[]{:S(2)}, u32[]{:S(2)}) collective-permute-start(bf16[544,128]{1,0:T(8,128)(2,1)} %get-tuple-element.32), channel_id=1, source_target_pairs={{0,64},{1,65},{2,66},{3,67},{4,68},{5,69},{6,70},{7,71},{8,72},{9,... | collective-permute-start | bytes 417800 | tf_op jit(solution)/shard_map/ppermute | solution.py:30
  11.5 18.7 %collective-permute-start.7 = (bf16[544,128]{1,0:T(8,128)(2,1)}, bf16[544,128]{1,0:T(8,128)(2,1)S(1)}, u32[]{:S(2)}, u32[]{:S(2)}) collective-permute-start(bf16[544,128]{1,0:T(8,128)(2,1)} %get-tuple-element.23.rest_0_), channel_id=1, source_target_pairs={{0,1},{1,0},{2,3},{3,2},{4,5},{5,4},{6,7},{7,6},{8,9},{9,8},{10,11... | collective-permute-start | bytes 417800 | tf_op jit(solution)/shard_map/ppermute | solution.py:30
  13.3 12.9 %copy-start.3 = (bf16[544,128]{1,0:T(8,128)(2,1)S(1)}, bf16[544,128]{1,0:T(8,128)(2,1)}, u32[]{:S(2)}) copy-start(bf16[544,128]{1,0:T(8,128)(2,1)} %get-tuple-element.36) | copy-start | bytes 417796
  13.3 16.9 %copy-start.2 = (bf16[544,128]{1,0:T(8,128)(2,1)S(1)}, bf16[544,128]{1,0:T(8,128)(2,1)}, u32[]{:S(2)}) copy-start(bf16[544,128]{1,0:T(8,128)(2,1)} %get-tuple-element.38) | copy-start | bytes 417796
  13.3 23.7 %copy-start.1 = (bf16[544,128]{1,0:T(8,128)(2,1)S(1)}, bf16[544,128]{1,0:T(8,128)(2,1)}, u32[]{:S(2)}) copy-start(bf16[544,128]{1,0:T(8,128)(2,1)} %get-tuple-element.23.rest_0_) | copy-start | bytes 417796
  13.3 25.7 %all-to-all-start = ((bf16[128,4,256]{2,1,0:T(4,128)(2,1)}), bf16[128,4,256]{2,1,0:T(4,128)(2,1)S(1)}, u32[]{:S(2)}, u32[]{:S(2)}) async-start(bf16[128,4,256]{2,1,0:T(4,128)(2,1)} %get-tuple-element.22), calls=%async_computation | async-start | bytes 524288 | tf_op jit(solution)/shard_map/all_to_all | solution.py:281
  24.7 6.8 %collective-permute-start.4 = (bf16[544,128]{1,0:T(8,128)(2,1)}, bf16[544,128]{1,0:T(8,128)(2,1)S(1)}, u32[]{:S(2)}, u32[]{:S(2)}) collective-permute-start(bf16[544,128]{1,0:T(8,128)(2,1)} %get-tuple-element.34), channel_id=1, source_target_pairs={{0,2},{1,3},{2,0},{3,1},{4,6},{5,7},{6,4},{7,5},{8,10},{9,11},{10,... | collective-permute-start | bytes 417800 | tf_op jit(solution)/shard_map/ppermute | solution.py:30
  26.2 4.1 %copy-start = (s32[256,1]{0,1:T(1,128)S(1)}, s32[256,1]{0,1:T(1,128)}, u32[]{:S(2)}) copy-start(s32[256,1]{0,1:T(1,128)} %param.8) | copy-start | bytes 3076
  26.2 8.2 %collective-permute-start.5 = (bf16[544,128]{1,0:T(8,128)(2,1)S(1)}, bf16[544,128]{1,0:T(8,128)(2,1)S(1)}, u32[]{:S(2)}, u32[]{:S(2)}) collective-permute-start(bf16[544,128]{1,0:T(8,128)(2,1)S(1)} %copy-done.3), channel_id=1, source_target_pairs={{0,96},{1,97},{2,98},{3,99},{4,100},{5,101},{6,102},{7,103},{8,104... | collective-permute-start | bytes 417800 | tf_op jit(solution)/shard_map/ppermute | solution.py:30
  29.2 1.9 %collective-permute-start.8 = (bf16[544,128]{1,0:T(8,128)(2,1)S(1)}, bf16[544,128]{1,0:T(8,128)(2,1)S(1)}, u32[]{:S(2)}, u32[]{:S(2)}) collective-permute-start(bf16[544,128]{1,0:T(8,128)(2,1)S(1)} %collective-permute-done.rest_1_), channel_id=1, source_target_pairs={{0,1},{1,0},{2,3},{3,2},{4,5},{5,4},{6,7},{7,6},{8,9},{9,8},{10,11... | collective-permute-start | bytes 417800 | tf_op jit(solution)/shard_map/ppermute | solution.py:30
  30.1 2.7 %collective-permute-start.9 = (bf16[544,128]{1,0:T(8,128)(2,1)S(1)}, bf16[544,128]{1,0:T(8,128)(2,1)S(1)}, u32[]{:S(2)}, u32[]{:S(2)}) collective-permute-start(bf16[544,128]{1,0:T(8,128)(2,1)S(1)} %collective-permute-done.1.rest_2_), channel_id=1, source_target_pairs={{0,1},{1,0},{2,3},{3,2},{4,5},{5,4},{6,7},{7,6},{8,9},{9,8},{10,11... | collective-permute-start | bytes 417800 | tf_op jit(solution)/shard_map/ppermute | solution.py:30
  30.2 5.6 %collective-permute-start.6 = (bf16[544,128]{1,0:T(8,128)(2,1)S(1)}, bf16[544,128]{1,0:T(8,128)(2,1)S(1)}, u32[]{:S(2)}, u32[]{:S(2)}) collective-permute-start(bf16[544,128]{1,0:T(8,128)(2,1)S(1)} %copy-done.2), channel_id=1, source_target_pairs={{0,32},{1,33},{2,34},{3,35},{4,36},{5,37},{6,38},{7,39},{8,40},{9,... | collective-permute-start | bytes 417800 | tf_op jit(solution)/shard_map/ppermute | solution.py:30
  31.1 7.9 %collective-permute-start.10 = (bf16[544,128]{1,0:T(8,128)(2,1)S(1)}, bf16[544,128]{1,0:T(8,128)(2,1)S(1)}, u32[]{:S(2)}, u32[]{:S(2)}) collective-permute-start(bf16[544,128]{1,0:T(8,128)(2,1)S(1)} %collective-permute-done.2.rest_3_), channel_id=1, source_target_pairs={{0,1},{1,0},{2,3},{3,2},{4,5},{5,4},{6,7},{7,6},{8,9},{9,8},{10,11... | collective-permute-start | bytes 417800 | tf_op jit(solution)/shard_map/ppermute | solution.py:30
  31.5 7.6 %collective-permute-start.11 = (bf16[544,128]{1,0:T(8,128)(2,1)S(1)}, bf16[544,128]{1,0:T(8,128)(2,1)S(1)}, u32[]{:S(2)}, u32[]{:S(2)}) collective-permute-start(bf16[544,128]{1,0:T(8,128)(2,1)S(1)} %collective-permute-done.3.rest_4_), channel_id=1, source_target_pairs={{0,1},{1,0},{2,3},{3,2},{4,5},{5,4},{6,7},{7,6},{8,9},{9,8},{10,11... | collective-permute-start | bytes 417800 | tf_op jit(solution)/shard_map/ppermute | solution.py:30
  32.8 6.2 %collective-permute-start.12 = (bf16[544,128]{1,0:T(8,128)(2,1)S(1)}, bf16[544,128]{1,0:T(8,128)(2,1)S(1)}, u32[]{:S(2)}, u32[]{:S(2)}) collective-permute-start(bf16[544,128]{1,0:T(8,128)(2,1)S(1)} %collective-permute-done.4.rest_5_), channel_id=1, source_target_pairs={{0,1},{1,0},{2,3},{3,2},{4,5},{5,4},{6,7},{7,6},{8,9},{9,8},{10,11... | collective-permute-start | bytes 417800 | tf_op jit(solution)/shard_map/ppermute | solution.py:30
  34.3 4.7 %collective-permute-start.13 = (bf16[544,128]{1,0:T(8,128)(2,1)S(1)}, bf16[544,128]{1,0:T(8,128)(2,1)S(1)}, u32[]{:S(2)}, u32[]{:S(2)}) collective-permute-start(bf16[544,128]{1,0:T(8,128)(2,1)S(1)} %collective-permute-done.5.rest_6_), channel_id=1, source_target_pairs={{0,1},{1,0},{2,3},{3,2},{4,5},{5,4},{6,7},{7,6},{8,9},{9,8},{10,11... | collective-permute-start | bytes 417800 | tf_op jit(solution)/shard_map/ppermute | solution.py:30
  35.9 3.2 %collective-permute-start.14 = (bf16[544,128]{1,0:T(8,128)(2,1)S(1)}, bf16[544,128]{1,0:T(8,128)(2,1)S(1)}, u32[]{:S(2)}, u32[]{:S(2)}) collective-permute-start(bf16[544,128]{1,0:T(8,128)(2,1)S(1)} %collective-permute-done.6.rest_7_), channel_id=1, source_target_pairs={{0,1},{1,0},{2,3},{3,2},{4,5},{5,4},{6,7},{7,6},{8,9},{9,8},{10,11... | collective-permute-start | bytes 417800 | tf_op jit(solution)/shard_map/ppermute | solution.py:30

commit v5 on v4

--- a/solution.py
+++ b/solution.py
@@ -241,11 +241,13 @@
     step = jnp.exp2(ahead(6))
     level = split(levels + ahead(2) + ahead(4))
     factor = jnp.exp2(level - jnp.max(level, axis=1, keepdims=True))
-    factor = factor / jnp.sum(factor, axis=1, keepdims=True) * split(step)
+    total = jnp.sum(factor, axis=1).reshape(16, 2, HEAD)
+    factor = factor * split(step)
     for v in range(4):
         at = 64 * (v // 2) + v % 2
         mean = split(parts_ref[:, :, v * HEAD : (v + 1) * HEAD])
         mean = jnp.sum(mean * factor[..., at : at + 1], axis=1).reshape(16, 2, HEAD)
+        mean = mean / total[..., at : at + 1]
         for pair in range(16):
             column = pair * 256 + v % 2 * HEAD
             whole[v // 2 * 2 : v // 2 * 2 + 2, column : column + HEAD] = mean[pair]

time: 68.8 us -> 68.8 us (level)
  no operation moved by 1% of the time
where the time goes in v5:
time: 68.8 us; the launch traced here: 68.6 us
  starting transfers between devices  31.2 us (45%)
  blocking collectives  22.9 us (33%)
  Pallas kernels  9.01 us (13%)
  waiting for transfers between devices  4.04 us (6%)
  between operations  0.79 us (1%)
    all_to_all x1, blocking collectives, per_device(): return combine(lax.all_to_all(partial, 'ctx', 0, 0).astype(jnp.float32))  22.9 us
    ppermute x15, starting transfers between devices, swap(): return lax.ppermute(array, 'ctx', [(i, i ^ mask) for i in range(DEVICES)])  19.8 us
    all_to_all x1, starting transfers between devices, per_device(): everyone = lax.all_to_all(send, 'ctx', 0, 0).reshape(DEVICES * SLOTS, 256)  11.4 us
    pallas_call x1, Pallas kernels, attend(): pl.pallas_call(attend_kernel, out_shape=jax.ShapeDtypeStruct((TOKENS, 640...  4.38 us
    pallas_call x1, Pallas kernels, pack(): pl.pallas_call(pack_kernel, out_shape=[jax.ShapeDtypeStruct((DEVICES, SLO...  2.54 us
    ppermute x15, waiting for transfers between devices, swap(): return lax.ppermute(array, 'ctx', [(i, i ^ mask) for i in range(DEVICES)])  2.44 us
    pallas_call x1, Pallas kernels, combine(): pl.pallas_call(combine_kernel, out_shape=jax.ShapeDtypeStruct((SLOTS, 409...  1.74 us
    all_to_all x1, waiting for transfers between devices, per_device(): everyone = lax.all_to_all(send, 'ctx', 0, 0).reshape(DEVICES * SLOTS, 256)  1.6 us
  transfers between devices with their start and end apart: 16, of which 4 were waited for; matrix products, arithmetic and copies ran while one was open for 0% of the time, Pallas kernels for 1%

profile of v5, /device:TPU:1, one launch (start us, length us, event | category | flops | bytes accessed | tf_op | source)
XLA Modules:
  0.0 68.6 jit_solution(6689808621495021324)
XLA Ops:
  0.7 2.5 %pack.1 = (bf16[128,4,256]{2,1,0:T(4,128)(2,1)}, bf16[544,128]{1,0:T(8,128)(2,1)}, bf16[544,128]{1,0:T(8,128)(2,1)}, bf16[544,128]{1,0:T(8,128)(2,1)}, bf16[544,...) custom-call(s32[1]{0:T(128)} %bitcast.head_ref, ...), custom_call_target="tpu_custom_call" | custom-call | bytes 2097152 | tf_op jit(solution)/shard_map/pack/pallas_call | solution.py:65
  3.2 3.1 %collective-permute-start.1 = (bf16[544,128]{1,0:T(8,128)(2,1)}, bf16[544,128]{1,0:T(8,128)(2,1)S(1)}, u32[]{:S(2)}, u32[]{:S(2)}) collective-permute-start(bf16[544,128]{1,0:T(8,128)(2,1)} %get-tuple-element.25), channel_id=1, source_target_pairs={{0,34},{1,35},{2,32},{3,33},{4,38},{5,39},{6,36},{7,37},{8,42},{9,... | collective-permute-start | bytes 417800 | tf_op jit(solution)/shard_map/ppermute | solution.py:30
  6.3 2.6 %collective-permute-start.2 = (bf16[544,128]{1,0:T(8,128)(2,1)}, bf16[544,128]{1,0:T(8,128)(2,1)S(1)}, u32[]{:S(2)}, u32[]{:S(2)}) collective-permute-start(bf16[544,128]{1,0:T(8,128)(2,1)} %get-tuple-element.26), channel_id=1, source_target_pairs={{0,66},{1,67},{2,64},{3,65},{4,70},{5,71},{6,68},{7,69},{8,74},{9,... | collective-permute-start | bytes 417800 | tf_op jit(solution)/shard_map/ppermute | solution.py:30
  8.9 0.9 %collective-permute-start = (bf16[544,128]{1,0:T(8,128)(2,1)}, bf16[544,128]{1,0:T(8,128)(2,1)S(1)}, u32[]{:S(2)}, u32[]{:S(2)}) collective-permute-start(bf16[544,128]{1,0:T(8,128)(2,1)} %get-tuple-element.24), channel_id=1, source_target_pairs={{0,98},{1,99},{2,96},{3,97},{4,102},{5,103},{6,100},{7,101},{8,106... | collective-permute-start | bytes 417800 | tf_op jit(solution)/shard_map/ppermute | solution.py:30
  9.8 1.7 %collective-permute-start.3 = (bf16[544,128]{1,0:T(8,128)(2,1)}, bf16[544,128]{1,0:T(8,128)(2,1)S(1)}, u32[]{:S(2)}, u32[]{:S(2)}) collective-permute-start(bf16[544,128]{1,0:T(8,128)(2,1)} %get-tuple-element.32), channel_id=1, source_target_pairs={{0,64},{1,65},{2,66},{3,67},{4,68},{5,69},{6,70},{7,71},{8,72},{9,... | collective-permute-start | bytes 417800 | tf_op jit(solution)/shard_map/ppermute | solution.py:30
  11.5 1.8 %collective-permute-start.7 = (bf16[544,128]{1,0:T(8,128)(2,1)}, bf16[544,128]{1,0:T(8,128)(2,1)S(1)}, u32[]{:S(2)}, u32[]{:S(2)}) collective-permute-start(bf16[544,128]{1,0:T(8,128)(2,1)} %get-tuple-element.23.rest_0_), channel_id=1, source_target_pairs={{0,1},{1,0},{2,3},{3,2},{4,5},{5,4},{6,7},{7,6},{8,9},{9,8},{10,11... | collective-permute-start | bytes 417800 | tf_op jit(solution)/shard_map/ppermute | solution.py:30
  13.3 11.4 %all-to-all-start = ((bf16[128,4,256]{2,1,0:T(4,128)(2,1)}), bf16[128,4,256]{2,1,0:T(4,128)(2,1)S(1)}, u32[]{:S(2)}, u32[]{:S(2)}) async-start(bf16[128,4,256]{2,1,0:T(4,128)(2,1)} %get-tuple-element.22), calls=%async_computation | async-start | bytes 524288 | tf_op jit(solution)/shard_map/all_to_all | solution.py:283
  24.7 1.5 %collective-permute-start.4 = (bf16[544,128]{1,0:T(8,128)(2,1)}, bf16[544,128]{1,0:T(8,128)(2,1)S(1)}, u32[]{:S(2)}, u32[]{:S(2)}) collective-permute-start(bf16[544,128]{1,0:T(8,128)(2,1)} %get-tuple-element.34), channel_id=1, source_target_pairs={{0,2},{1,3},{2,0},{3,1},{4,6},{5,7},{6,4},{7,5},{8,10},{9,11},{10,... | collective-permute-start | bytes 417800 | tf_op jit(solution)/shard_map/ppermute | solution.py:30
  26.2 0.0 collective-permute-done.2.rest_3_
  26.2 3.0 %collective-permute-start.5 = (bf16[544,128]{1,0:T(8,128)(2,1)S(1)}, bf16[544,128]{1,0:T(8,128)(2,1)S(1)}, u32[]{:S(2)}, u32[]{:S(2)}) collective-permute-start(bf16[544,128]{1,0:T(8,128)(2,1)S(1)} %copy-done.3), channel_id=1, source_target_pairs={{0,96},{1,97},{2,98},{3,99},{4,100},{5,101},{6,102},{7,103},{8,104... | collective-permute-start | bytes 417800 | tf_op jit(solution)/shard_map/ppermute | solution.py:30
  29.2 0.0 collective-permute-done.rest_1_
  29.2 0.9 %collective-permute-start.8 = (bf16[544,128]{1,0:T(8,128)(2,1)S(1)}, bf16[544,128]{1,0:T(8,128)(2,1)S(1)}, u32[]{:S(2)}, u32[]{:S(2)}) collective-permute-start(bf16[544,128]{1,0:T(8,128)(2,1)S(1)} %collective-permute-done.rest_1_), channel_id=1, source_target_pairs={{0,1},{1,0},{2,3},{3,2},{4,5},{5,4},{6,7},{7,6},{8,9},{9,8},{10,11... | collective-permute-start | bytes 417800 | tf_op jit(solution)/shard_map/ppermute | solution.py:30
  30.1 0.0 collective-permute-done.3.rest_4_
  30.1 0.1 collective-permute-start.9
  30.2 0.0 collective-permute-start.6
  30.3 0.1 copy.8.col_ref
  30.4 0.7 %collective-permute-done.8.rest_9_ = bf16[544,128]{1,0:T(8,128)(2,1)S(1)} collective-permute-done((bf16[544,128]{1,0:T(8,128)(2,1)S(1)}, bf16[544,128]{1,0:T(8,128)(2,1)S(1)}, u32[]{:S(2)}, u32[]{:S(2)}) %collective-permute-start.8) | collective-permute-done | bytes 139296 | tf_op jit(solution)/shard_map/ppermute | solution.py:30
  31.1 0.4 collective-permute-start.10
  31.5 1.3 %collective-permute-start.11 = (bf16[544,128]{1,0:T(8,128)(2,1)S(1)}, bf16[544,128]{1,0:T(8,128)(2,1)S(1)}, u32[]{:S(2)}, u32[]{:S(2)}) collective-permute-start(bf16[544,128]{1,0:T(8,128)(2,1)S(1)} %collective-permute-done.3.rest_4_), channel_id=1, source_target_pairs={{0,1},{1,0},{2,3},{3,2},{4,5},{5,4},{6,7},{7,6},{8,9},{9,8},{10,11... | collective-permute-start | bytes 417800 | tf_op jit(solution)/shard_map/ppermute | solution.py:30
  32.8 0.0 collective-permute-start.12
  32.8 1.5 %collective-permute-done.5.rest_6_ = bf16[544,128]{1,0:T(8,128)(2,1)S(1)} collective-permute-done((bf16[544,128]{1,0:T(8,128)(2,1)S(1)}, bf16[544,128]{1,0:T(8,128)(2,1)S(1)}, u32[]{:S(2)}, u32[]{:S(2)}) %collective-permute-start.5) | collective-permute-done | bytes 139296 | tf_op jit(solution)/shard_map/ppermute | solution.py:30
  34.3 1.3 %collective-permute-start.13 = (bf16[544,128]{1,0:T(8,128)(2,1)S(1)}, bf16[544,128]{1,0:T(8,128)(2,1)S(1)}, u32[]{:S(2)}, u32[]{:S(2)}) collective-permute-start(bf16[544,128]{1,0:T(8,128)(2,1)S(1)} %collective-permute-done.5.rest_6_), channel_id=1, source_target_pairs={{0,1},{1,0},{2,3},{3,2},{4,5},{5,4},{6,7},{7,6},{8,9},{9,8},{10,11... | collective-permute-start | bytes 417800 | tf_op jit(solution)/shard_map/ppermute | solution.py:30
  35.7 0.2 collective-permute-done.6.rest_7_
  35.9 1.1 %collective-permute-start.14 = (bf16[544,128]{1,0:T(8,128)(2,1)S(1)}, bf16[544,128]{1,0:T(8,128)(2,1)S(1)}, u32[]{:S(2)}, u32[]{:S(2)}) collective-permute-start(bf16[544,128]{1,0:T(8,128)(2,1)S(1)} %collective-permute-done.6.rest_7_), channel_id=1, source_target_pairs={{0,1},{1,0},{2,3},{3,2},{4,5},{5,4},{6,7},{7,6},{8,9},{9,8},{10,11... | collective-permute-start | bytes 417800 | tf_op jit(solution)/shard_map/ppermute | solution.py:30
  37.0 0.4 prepare.1
  37.4 1.6 %all-to-all-done = bf16[128,4,256]{2,1,0:T(4,128)(2,1)S(1)} async-done(((bf16[128,4,256]{2,1,0:T(4,128)(2,1)}), bf16[128,4,256]{2,1,0:T(4,128)(2,1)S(1)}, u32[]{:S(2)}, u32[]{:S(2)}) %all-to-all-start) | async-done | bytes 262176 | tf_op jit(solution)/shard_map/all_to_all | solution.py:283
  39.0 0.1 reshape.9.q_ref
  39.1 4.4 %attend.1 = f32[256,640]{1,0:T(8,128)S(1)} custom-call(bf16[512,256]{1,0:T(8,128)(2,1)S(1)} %reshape.9.q_ref, bf16[256,512]{1,0:T(8,128)(2,1)S(1)} %get-tuple-element.27.pick, bf16[256,256]{1,0:T(8,128)(2,1)S(1)} %get-tuple-element.28.near, bf16[256,256]{1,0:T(8,128)(2,1)S(1)} %get-tuple-element.29.far, f32[1,256]{1,0:T(1,128)S(1)} %get-tuple-element.30.token_ref, ...), custom_call_target="tpu_custom_call" | custom-call | flops 1140850688 | bytes 3145728 | tf_op jit(solution)/shard_map/attend/pallas_call | solution.py:219
  43.5 0.2 reshape.11
  43.7 22.9 %all_to_all.10 = f16[128,2,640]{2,1,0:T(2,128)(2,1)S(1)} all-to-all(f16[128,2,640]{2,1,0:T(2,128)(2,1)S(1)} %reshape.11), channel_id=1, replica_groups=mesh['batch'=2,'ctx'=128] {'ctx'}, dimensions={0} | all-to-all | bytes 655360 | tf_op jit(solution)/shard_map/all_to_all | solution.py:287
  66.6 0.2 convert_element_type.7.parts_ref
  66.9 1.7 %combine.1 = bf16[4,4096]{1,0:T(4,128)(2,1)} custom-call(f32[128,2,640]{2,1,0:T(2,128)S(1)} %convert_element_type.7.parts_ref), custom_call_target="tpu_custom_call" | custom-call | tf_op jit(solution)/shard_map/combine/pallas_call | solution.py:259
  (18 shorter events, 0.1 us)
Async XLA Ops:
  3.2 21.5 %collective-permute-start.1 = (bf16[544,128]{1,0:T(8,128)(2,1)}, bf16[544,128]{1,0:T(8,128)(2,1)S(1)}, u32[]{:S(2)}, u32[]{:S(2)}) collective-permute-start(bf16[544,128]{1,0:T(8,128)(2,1)} %get-tuple-element.25), channel_id=1, source_target_pairs={{0,34},{1,35},{2,32},{3,33},{4,38},{5,39},{6,36},{7,37},{8,42},{9,... | collective-permute-start | bytes 417800 | tf_op jit(solution)/shard_map/ppermute | solution.py:30
  6.3 19.8 %collective-permute-start.2 = (bf16[544,128]{1,0:T(8,128)(2,1)}, bf16[544,128]{1,0:T(8,128)(2,1)S(1)}, u32[]{:S(2)}, u32[]{:S(2)}) collective-permute-start(bf16[544,128]{1,0:T(8,128)(2,1)} %get-tuple-element.26), channel_id=1, source_target_pairs={{0,66},{1,67},{2,64},{3,65},{4,70},{5,71},{6,68},{7,69},{8,74},{9,... | collective-permute-start | bytes 417800 | tf_op jit(solution)/shard_map/ppermute | solution.py:30
  8.9 20.3 %collective-permute-start = (bf16[544,128]{1,0:T(8,128)(2,1)}, bf16[544,128]{1,0:T(8,128)(2,1)S(1)}, u32[]{:S(2)}, u32[]{:S(2)}) collective-permute-start(bf16[544,128]{1,0:T(8,128)(2,1)} %get-tuple-element.24), channel_id=1, source_target_pairs={{0,98},{1,99},{2,96},{3,97},{4,102},{5,103},{6,100},{7,101},{8,106... | collective-permute-start | bytes 417800 | tf_op jit(solution)/shard_map/ppermute | solution.py:30
  9.8 20.3 %collective-permute-start.3 = (bf16[544,128]{1,0:T(8,128)(2,1)}, bf16[544,128]{1,0:T(8,128)(2,1)S(1)}, u32[]{:S(2)}, u32[]{:S(2)}) collective-permute-start(bf16[544,128]{1,0:T(8,128)(2,1)} %get-tuple-element.32), channel_id=1, source_target_pairs={{0,64},{1,65},{2,66},{3,67},{4,68},{5,69},{6,70},{7,71},{8,72},{9,... | collective-permute-start | bytes 417800 | tf_op jit(solution)/shard_map/ppermute | solution.py:30
  11.5 18.7 %collective-permute-start.7 = (bf16[544,128]{1,0:T(8,128)(2,1)}, bf16[544,128]{1,0:T(8,128)(2,1)S(1)}, u32[]{:S(2)}, u32[]{:S(2)}) collective-permute-start(bf16[544,128]{1,0:T(8,128)(2,1)} %get-tuple-element.23.rest_0_), channel_id=1, source_target_pairs={{0,1},{1,0},{2,3},{3,2},{4,5},{5,4},{6,7},{7,6},{8,9},{9,8},{10,11... | collective-permute-start | bytes 417800 | tf_op jit(solution)/shard_map/ppermute | solution.py:30
  13.3 12.9 %copy-start.3 = (bf16[544,128]{1,0:T(8,128)(2,1)S(1)}, bf16[544,128]{1,0:T(8,128)(2,1)}, u32[]{:S(2)}) copy-start(bf16[544,128]{1,0:T(8,128)(2,1)} %get-tuple-element.36) | copy-start | bytes 417796
  13.3 16.9 %copy-start.2 = (bf16[544,128]{1,0:T(8,128)(2,1)S(1)}, bf16[544,128]{1,0:T(8,128)(2,1)}, u32[]{:S(2)}) copy-start(bf16[544,128]{1,0:T(8,128)(2,1)} %get-tuple-element.38) | copy-start | bytes 417796
  13.3 23.7 %copy-start.1 = (bf16[544,128]{1,0:T(8,128)(2,1)S(1)}, bf16[544,128]{1,0:T(8,128)(2,1)}, u32[]{:S(2)}) copy-start(bf16[544,128]{1,0:T(8,128)(2,1)} %get-tuple-element.23.rest_0_) | copy-start | bytes 417796
  13.3 25.7 %all-to-all-start = ((bf16[128,4,256]{2,1,0:T(4,128)(2,1)}), bf16[128,4,256]{2,1,0:T(4,128)(2,1)S(1)}, u32[]{:S(2)}, u32[]{:S(2)}) async-start(bf16[128,4,256]{2,1,0:T(4,128)(2,1)} %get-tuple-element.22), calls=%async_computation | async-start | bytes 524288 | tf_op jit(solution)/shard_map/all_to_all | solution.py:283
  24.7 6.8 %collective-permute-start.4 = (bf16[544,128]{1,0:T(8,128)(2,1)}, bf16[544,128]{1,0:T(8,128)(2,1)S(1)}, u32[]{:S(2)}, u32[]{:S(2)}) collective-permute-start(bf16[544,128]{1,0:T(8,128)(2,1)} %get-tuple-element.34), channel_id=1, source_target_pairs={{0,2},{1,3},{2,0},{3,1},{4,6},{5,7},{6,4},{7,5},{8,10},{9,11},{10,... | collective-permute-start | bytes 417800 | tf_op jit(solution)/shard_map/ppermute | solution.py:30
  26.2 4.1 %copy-start = (s32[256,1]{0,1:T(1,128)S(1)}, s32[256,1]{0,1:T(1,128)}, u32[]{:S(2)}) copy-start(s32[256,1]{0,1:T(1,128)} %param.8) | copy-start | bytes 3076
  26.2 8.2 %collective-permute-start.5 = (bf16[544,128]{1,0:T(8,128)(2,1)S(1)}, bf16[544,128]{1,0:T(8,128)(2,1)S(1)}, u32[]{:S(2)}, u32[]{:S(2)}) collective-permute-start(bf16[544,128]{1,0:T(8,128)(2,1)S(1)} %copy-done.3), channel_id=1, source_target_pairs={{0,96},{1,97},{2,98},{3,99},{4,100},{5,101},{6,102},{7,103},{8,104... | collective-permute-start | bytes 417800 | tf_op jit(solution)/shard_map/ppermute | solution.py:30
  29.2 1.9 %collective-permute-start.8 = (bf16[544,128]{1,0:T(8,128)(2,1)S(1)}, bf16[544,128]{1,0:T(8,128)(2,1)S(1)}, u32[]{:S(2)}, u32[]{:S(2)}) collective-permute-start(bf16[544,128]{1,0:T(8,128)(2,1)S(1)} %collective-permute-done.rest_1_), channel_id=1, source_target_pairs={{0,1},{1,0},{2,3},{3,2},{4,5},{5,4},{6,7},{7,6},{8,9},{9,8},{10,11... | collective-permute-start | bytes 417800 | tf_op jit(solution)/shard_map/ppermute | solution.py:30
  30.1 2.7 %collective-permute-start.9 = (bf16[544,128]{1,0:T(8,128)(2,1)S(1)}, bf16[544,128]{1,0:T(8,128)(2,1)S(1)}, u32[]{:S(2)}, u32[]{:S(2)}) collective-permute-start(bf16[544,128]{1,0:T(8,128)(2,1)S(1)} %collective-permute-done.1.rest_2_), channel_id=1, source_target_pairs={{0,1},{1,0},{2,3},{3,2},{4,5},{5,4},{6,7},{7,6},{8,9},{9,8},{10,11... | collective-permute-start | bytes 417800 | tf_op jit(solution)/shard_map/ppermute | solution.py:30
  30.2 5.6 %collective-permute-start.6 = (bf16[544,128]{1,0:T(8,128)(2,1)S(1)}, bf16[544,128]{1,0:T(8,128)(2,1)S(1)}, u32[]{:S(2)}, u32[]{:S(2)}) collective-permute-start(bf16[544,128]{1,0:T(8,128)(2,1)S(1)} %copy-done.2), channel_id=1, source_target_pairs={{0,32},{1,33},{2,34},{3,35},{4,36},{5,37},{6,38},{7,39},{8,40},{9,... | collective-permute-start | bytes 417800 | tf_op jit(solution)/shard_map/ppermute | solution.py:30
  31.1 7.9 %collective-permute-start.10 = (bf16[544,128]{1,0:T(8,128)(2,1)S(1)}, bf16[544,128]{1,0:T(8,128)(2,1)S(1)}, u32[]{:S(2)}, u32[]{:S(2)}) collective-permute-start(bf16[544,128]{1,0:T(8,128)(2,1)S(1)} %collective-permute-done.2.rest_3_), channel_id=1, source_target_pairs={{0,1},{1,0},{2,3},{3,2},{4,5},{5,4},{6,7},{7,6},{8,9},{9,8},{10,11... | collective-permute-start | bytes 417800 | tf_op jit(solution)/shard_map/ppermute | solution.py:30
  31.5 7.6 %collective-permute-start.11 = (bf16[544,128]{1,0:T(8,128)(2,1)S(1)}, bf16[544,128]{1,0:T(8,128)(2,1)S(1)}, u32[]{:S(2)}, u32[]{:S(2)}) collective-permute-start(bf16[544,128]{1,0:T(8,128)(2,1)S(1)} %collective-permute-done.3.rest_4_), channel_id=1, source_target_pairs={{0,1},{1,0},{2,3},{3,2},{4,5},{5,4},{6,7},{7,6},{8,9},{9,8},{10,11... | collective-permute-start | bytes 417800 | tf_op jit(solution)/shard_map/ppermute | solution.py:30
  32.8 6.2 %collective-permute-start.12 = (bf16[544,128]{1,0:T(8,128)(2,1)S(1)}, bf16[544,128]{1,0:T(8,128)(2,1)S(1)}, u32[]{:S(2)}, u32[]{:S(2)}) collective-permute-start(bf16[544,128]{1,0:T(8,128)(2,1)S(1)} %collective-permute-done.4.rest_5_), channel_id=1, source_target_pairs={{0,1},{1,0},{2,3},{3,2},{4,5},{5,4},{6,7},{7,6},{8,9},{9,8},{10,11... | collective-permute-start | bytes 417800 | tf_op jit(solution)/shard_map/ppermute | solution.py:30
  34.3 4.7 %collective-permute-start.13 = (bf16[544,128]{1,0:T(8,128)(2,1)S(1)}, bf16[544,128]{1,0:T(8,128)(2,1)S(1)}, u32[]{:S(2)}, u32[]{:S(2)}) collective-permute-start(bf16[544,128]{1,0:T(8,128)(2,1)S(1)} %collective-permute-done.5.rest_6_), channel_id=1, source_target_pairs={{0,1},{1,0},{2,3},{3,2},{4,5},{5,4},{6,7},{7,6},{8,9},{9,8},{10,11... | collective-permute-start | bytes 417800 | tf_op jit(solution)/shard_map/ppermute | solution.py:30
  35.9 3.2 %collective-permute-start.14 = (bf16[544,128]{1,0:T(8,128)(2,1)S(1)}, bf16[544,128]{1,0:T(8,128)(2,1)S(1)}, u32[]{:S(2)}, u32[]{:S(2)}) collective-permute-start(bf16[544,128]{1,0:T(8,128)(2,1)S(1)} %collective-permute-done.6.rest_7_), channel_id=1, source_target_pairs={{0,1},{1,0},{2,3},{3,2},{4,5},{5,4},{6,7},{7,6},{8,9},{9,8},{10,11... | collective-permute-start | bytes 417800 | tf_op jit(solution)/shard_map/ppermute | solution.py:30
